TPU v7x, 32 devices: a whole 2x2x4 slice. The times are simulated.
32 devices in a mesh: dp: 8 (over z, y), narrow: 4 (over x, core).
Axes of the slice: x: 2, y: 2, z: 4, core: 2. Of those that a mesh axis runs over, the one named last changes fastest.
Arguments:
- tokens: bfloat16 [25088, 768], P(('dp', 'narrow')), may hold values from -6 to 6
- input_projection: bfloat16 [3, 768, 768], P(None, None, 'narrow'), may hold values from -0.21875 to 0.21875
- input_bias: float32 [2, 768], replicated, may hold values from -3 to 3
- position_bias: float32 [169, 24], replicated, may hold values from -4 to 4
- output_projection: bfloat16 [768, 768], P('narrow'), may hold values from -0.5 to 0.5
- inner_weight: bfloat16 [768, 3072], P(None, 'narrow'), may hold values from -0.21875 to 0.21875
- inner_bias: float32 [3072], replicated, may hold values from -2 to 2
- outer_weight: bfloat16 [3072, 768], P('narrow'), may hold values from -0.109375 to 0.109375
- norm_gains: float32 [3, 768], replicated, may hold values from 0.5 to 1.5
- offsets: float32 [5, 768], replicated, may hold values from -2 to 2
- head_first: bfloat16 [768, 2048], replicated, may hold values from -0.21875 to 0.21875
- head_first_bias: float32 [2048], replicated, may hold values from -2 to 2
- head_second: bfloat16 [2048, 2048], replicated, may hold values from -0.125 to 0.125
- head_second_bias: float32 [2048], replicated, may hold values from -2 to 2
- head_third: bfloat16 [2048, 256], replicated, may hold values from -0.125 to 0.125
- head_third_bias: float32 [256], replicated, may hold values from -2 to 2
- prototype_direction: bfloat16 [256, 65536], P(None, ('dp', 'narrow')), may hold values from -6 to 6
- prototype_gain: float32 [65536], P(('dp', 'narrow')), may hold values from 10 to 40
- crop_windows: int32 [8, 4], P('dp'), may hold values from 1 to 49, as said below
- first_epoch: int32 [65536], P(('dp', 'narrow')), may hold values 0 or 1
- feature_cotangent: bfloat16 [25088, 768], P(('dp', 'narrow')), may hold values from -6 to 6
- logit_cotangent: bfloat16 [32, 65536], P(None, ('dp', 'narrow')), may hold values from -6 to 6
Outputs:
- features: bfloat16 [25088, 768], P(('dp', 'narrow'))
- logits: float32 [32, 65536], P(None, ('dp', 'narrow'))
- tokens_grad: float32 [25088, 768], P(('dp', 'narrow'))
- input_projection_grad: float32 [3, 768, 768], P(None, 'dp', 'narrow')
- input_bias_grad: float32 [2, 768], replicated
- position_bias_grad: float32 [169, 24], replicated
- output_projection_grad: float32 [768, 768], P('narrow', 'dp')
- inner_weight_grad: float32 [768, 3072], P('dp', 'narrow')
- inner_bias_grad: float32 [3072], replicated
- outer_weight_grad: float32 [3072, 768], P('narrow', 'dp')
- norm_gains_grad: float32 [3, 768], replicated
- offsets_grad: float32 [5, 768], replicated
- head_first_grad: float32 [768, 2048], P(None, 'dp')
- head_first_bias_grad: float32 [2048], P('dp')
- head_second_grad: float32 [2048, 2048], P(None, 'dp')
- head_second_bias_grad: float32 [2048], P('dp')
- head_third_grad: float32 [2048, 256], P('dp')
- head_third_bias_grad: float32 [256], P('dp')
- prototype_direction_grad: float32 [256, 65536], P(None, ('dp', 'narrow'))
- prototype_gain_grad: float32 [65536], P(('dp', 'narrow'))
Inputs may be any that keep to these rules, and one draw needn't show every extreme that they name: `crop_windows`: each row sums to 64; one entry of each row, at a place drawn from the seed, is exactly 49, and the others sum to 15.
All inputs are finite; a program needn't handle non-finite values. No bound on the sum of `first_epoch` on one device may be relied on, other than what follows from the above.
Results may differ from a plain program's by a relative error of at most 0.017.
The roundings to bfloat16 on the way count: a program that leaves them out, or rounds other values in their place, can miss the bound.
Values may be sent and summed in bfloat16 or wider, within the bound.
No kernel may reach another device: no remote copies, remote signals or barrier semaphores. Data moves between devices by JAX's collectives and lax.ppermute only.
A program may use at most 192 MiB of HBM per device.

v0:
```python
import jax
import jax.numpy as jnp
from jax import lax
from jax.sharding import PartitionSpec as P

HIGH = lax.Precision.HIGHEST
window_side = 7


def layer_norm(values, gain, shift):
    center = values - jnp.mean(values, axis=-1, keepdims=True)
    spread = jnp.mean(center * center, axis=-1, keepdims=True)
    return center * lax.rsqrt(spread + 1e-05) * gain + shift


def gelu_exact(values):
    return jax.nn.gelu(values, approximate=False)


def normalize_rows(values):
    return values * lax.rsqrt(jnp.sum(values * values, axis=-1, keepdims=True) + 1e-06)


def offset_table():
    places = jnp.arange(window_side * window_side, dtype=jnp.int32)
    row_of = places // window_side
    col_of = places % window_side
    offset = (row_of[:, None] - row_of[None, :] + window_side - 1) * (2 * window_side - 1) + (
        col_of[:, None] - col_of[None, :] + window_side - 1
    )
    entries = jnp.arange((2 * window_side - 1) ** 2, dtype=jnp.int32)
    return (offset.reshape(-1)[:, None] == entries[None, :]).astype(jnp.float32)


def product(left, right):
    return jnp.dot(left, right, preferred_element_type=jnp.float32)


def product_high(left, right):
    return jnp.dot(left, right, precision=HIGH, preferred_element_type=jnp.float32)


def product_left(left, right):
    return lax.dot_general(
        left, right, (((0,), (0,)), ((), ())), preferred_element_type=jnp.float32
    )


def product_high_left(left, right):
    return lax.dot_general(
        left, right, (((0,), (0,)), ((), ())), precision=HIGH, preferred_element_type=jnp.float32
    )


def product_right(left, right):
    return lax.dot_general(
        left, right, (((1,), (1,)), ((), ())), preferred_element_type=jnp.float32
    )


def gelu_back(pre, cotangent):
    return jax.vjp(gelu_exact, pre)[1](cotangent)[0]


def head_forward(pooled, weights):
    first, first_bias, second, second_bias, third, third_bias = weights
    pooled_low = pooled.astype(jnp.bfloat16)
    first_pre = product(pooled_low, first) + first_bias
    first_act = gelu_exact(first_pre).astype(jnp.bfloat16)
    second_pre = product(first_act, second) + second_bias
    second_act = gelu_exact(second_pre).astype(jnp.bfloat16)
    embedded = product(second_act, third) + third_bias
    units = normalize_rows(embedded).astype(jnp.bfloat16)
    return ((pooled_low, first_pre, first_act, second_pre, second_act, embedded), units)


def head_backward(kept, unit_cotangent, weights):
    pooled_low, first_pre, first_act, second_pre, second_act, embedded = kept
    first = weights[0]
    second = weights[2]
    third = weights[4]
    embed_grad = jax.vjp(normalize_rows, embedded)[1](unit_cotangent)[0]
    embed_low = embed_grad.astype(jnp.bfloat16)
    third_grad = product_left(second_act, embed_low)
    third_bias_grad = jnp.sum(embed_grad, axis=0)
    second_low = gelu_back(second_pre, product_right(embed_low, third)).astype(jnp.bfloat16)
    second_grad = product_left(first_act, second_low)
    second_bias_grad = jnp.sum(second_low.astype(jnp.float32), axis=0)
    first_low = gelu_back(first_pre, product_right(second_low, second)).astype(jnp.bfloat16)
    first_grad = product_left(pooled_low, first_low)
    first_bias_grad = jnp.sum(first_low.astype(jnp.float32), axis=0)
    pooled_grad = product_right(first_low, first)
    return (
        (first_grad, first_bias_grad, second_grad, second_bias_grad, third_grad, third_bias_grad),
        pooled_grad,
    )


def shards(
    tokens,
    input_projection,
    input_bias,
    position_bias,
    output_projection,
    inner_weight,
    inner_bias,
    outer_weight,
    norm_gains,
    offsets,
    head_first,
    head_first_bias,
    head_second,
    head_second_bias,
    head_third,
    head_third_bias,
    prototype_direction,
    prototype_gain,
    crop_windows,
    first_epoch,
    feature_cotangent,
    logit_cotangent,
):
    rows = tokens.shape[0]
    narrow_index = lax.axis_index("narrow")
    dp_index = lax.axis_index("dp")
    narrow_count = lax.axis_size("narrow")
    head_weights = (
        head_first,
        head_first_bias,
        head_second,
        head_second_bias,
        head_third,
        head_third_bias,
    )
    inputs = tokens.astype(jnp.float32)
    normed_one = layer_norm(inputs, norm_gains[0], offsets[0])
    attend_in = lax.all_gather(normed_one.astype(jnp.bfloat16), "narrow", axis=0, tiled=True)
    share = input_projection.shape[2]
    head_share = position_bias.shape[1] // narrow_count
    bias_in = lax.dynamic_slice_in_dim(input_bias, narrow_index * share, share, 1)
    bias_inner = lax.dynamic_slice_in_dim(
        inner_bias, narrow_index * inner_weight.shape[1], inner_weight.shape[1], 0
    )
    table_share = lax.dynamic_slice_in_dim(position_bias, narrow_index * head_share, head_share, 1)
    local_width = input_projection.shape[2]
    local_heads = table_share.shape[1]
    head_size = local_width // local_heads
    scale = head_size ** (-0.5)
    group_rows = attend_in.shape[0]
    group_windows = group_rows // 49
    query_rows = (product(attend_in, input_projection[0]) + bias_in[0]).astype(jnp.bfloat16)
    key_rows = product(attend_in, input_projection[1]).astype(jnp.bfloat16)
    value_rows = (product(attend_in, input_projection[2]) + bias_in[1]).astype(jnp.bfloat16)

    def windowed(values):
        return values.reshape(group_windows, 49, local_heads, head_size)

    table = offset_table()
    pair_bias = product_high(table, table_share).T.reshape(local_heads, 49, 49)

    def score_block():
        raw = jnp.einsum(
            "wihd,wjhd->whij",
            windowed(query_rows),
            windowed(key_rows),
            preferred_element_type=jnp.float32,
        )
        return raw * scale + pair_bias

    scores = score_block()
    top = jnp.max(scores, axis=-1, keepdims=True)
    log_total = top + jnp.log(jnp.sum(jnp.exp(scores - top), axis=-1, keepdims=True))
    probs = jnp.exp(scores - log_total).astype(jnp.bfloat16)
    attended = jnp.einsum(
        "whij,wjhd->wihd", probs, windowed(value_rows), preferred_element_type=jnp.float32
    )
    attended = attended.reshape(group_rows, local_width).astype(jnp.bfloat16)
    attend_out = lax.psum_scatter(
        product(attended, output_projection).astype(jnp.bfloat16),
        "narrow",
        scatter_dimension=0,
        tiled=True,
    ).astype(jnp.float32)
    mixed = inputs + attend_out + offsets[1]
    normed_two = layer_norm(mixed, norm_gains[1], offsets[2])
    inner_in = lax.all_gather(normed_two.astype(jnp.bfloat16), "narrow", axis=0, tiled=True)
    inner_pre = product(inner_in, inner_weight) + bias_inner
    inner_act = gelu_exact(inner_pre).astype(jnp.bfloat16)
    mlp_out = lax.psum_scatter(
        product(inner_act, outer_weight).astype(jnp.bfloat16),
        "narrow",
        scatter_dimension=0,
        tiled=True,
    ).astype(jnp.float32)
    block_out = mixed + mlp_out + offsets[3]
    normed_head = layer_norm(block_out, norm_gains[2], offsets[4])
    crop_count = crop_windows.shape[1]
    ends = jnp.cumsum(crop_windows[0])
    window_ids = narrow_index * (rows // 49) + jnp.arange(rows // 49, dtype=jnp.int32)
    crop_of_window = jnp.sum((window_ids[:, None] >= ends[None, :]).astype(jnp.int32), axis=1)
    window_member = (
        crop_of_window[:, None] == jnp.arange(crop_count, dtype=jnp.int32)[None, :]
    ).astype(jnp.float32)
    token_member = jnp.repeat(window_member, 49, axis=0)
    partial_pool = product_high_left(token_member, normed_head)
    crop_tokens = (crop_windows[0] * 49).astype(jnp.float32)
    pooled_sum = lax.psum(partial_pool, "narrow")
    kept, own_units = head_forward(pooled_sum / crop_tokens[:, None], head_weights)
    units = lax.all_gather(own_units, "dp", axis=0, tiled=True)

    def normalized(direction_in, gain_in):
        column_scale = lax.rsqrt(
            jnp.sum(direction_in * direction_in, axis=0, keepdims=True) + 1e-06
        )
        return gain_in * direction_in * column_scale

    columns, column_back = jax.vjp(
        normalized, prototype_direction.astype(jnp.float32), prototype_gain
    )
    columns_low = columns.astype(jnp.bfloat16)
    logits = product(units, columns_low)
    keep_flags = (1 - first_epoch).astype(jnp.float32)
    direction_grad, gain_grad = column_back(product_left(units, logit_cotangent))
    direction_grad = direction_grad * keep_flags[None, :]
    gain_grad = gain_grad * keep_flags
    unit_grad = lax.psum(product_right(logit_cotangent, columns_low), ("dp", "narrow"))
    own_grad = lax.dynamic_slice_in_dim(unit_grad, dp_index * crop_count, crop_count, 0)
    head_grads, pooled_grad = head_backward(kept, own_grad, head_weights)
    normed_head_grad = product_high(token_member, pooled_grad / crop_tokens[:, None])
    head_back = jax.vjp(layer_norm, block_out, norm_gains[2], offsets[4])[1](normed_head_grad)
    out_grad = feature_cotangent.astype(jnp.float32) + head_back[0]
    outer_bias_grad = jnp.sum(out_grad, axis=0)
    outer_rows = lax.all_gather(out_grad.astype(jnp.bfloat16), "narrow", axis=0, tiled=True)
    outer_grad = product_left(inner_act, outer_rows)
    pre_grad = gelu_back(inner_pre, product_right(outer_rows, outer_weight)).astype(jnp.bfloat16)
    inner_grad = product_left(inner_in, pre_grad)
    inner_bias_grad = jnp.sum(pre_grad.astype(jnp.float32), axis=0)
    normed_two_grad = lax.psum_scatter(
        product_right(pre_grad, inner_weight).astype(jnp.bfloat16),
        "narrow",
        scatter_dimension=0,
        tiled=True,
    ).astype(jnp.float32)
    two_back = jax.vjp(layer_norm, mixed, norm_gains[1], offsets[2])[1](normed_two_grad)
    mixed_grad = out_grad + two_back[0]
    attend_bias_grad = jnp.sum(mixed_grad, axis=0)
    attend_rows = lax.all_gather(mixed_grad.astype(jnp.bfloat16), "narrow", axis=0, tiled=True)
    output_grad = product_left(attended, attend_rows)
    attended_grad = product_right(attend_rows, output_projection).astype(jnp.bfloat16)
    again = jnp.exp(score_block() - log_total)
    grad_windows = windowed(attended_grad)
    value_grad = jnp.einsum(
        "whij,wihd->wjhd",
        again.astype(jnp.bfloat16),
        grad_windows,
        preferred_element_type=jnp.float32,
    )
    value_grad = value_grad.reshape(group_rows, local_width).astype(jnp.bfloat16)
    prob_grad = jnp.einsum(
        "wihd,wjhd->whij", grad_windows, windowed(value_rows), preferred_element_type=jnp.float32
    )
    score_grad = (again * (prob_grad - jnp.sum(again * prob_grad, axis=-1, keepdims=True))).astype(
        jnp.bfloat16
    )
    pair_grad = jnp.sum(score_grad.astype(jnp.float32), axis=0).reshape(local_heads, 49 * 49)
    table_grad = product_high_left(table, pair_grad.T)
    query_grad = (
        jnp.einsum(
            "whij,wjhd->wihd", score_grad, windowed(key_rows), preferred_element_type=jnp.float32
        )
        * scale
    )
    query_grad = query_grad.reshape(group_rows, local_width).astype(jnp.bfloat16)
    key_grad = (
        jnp.einsum(
            "whij,wihd->wjhd", score_grad, windowed(query_rows), preferred_element_type=jnp.float32
        )
        * scale
    )
    key_grad = key_grad.reshape(group_rows, local_width).astype(jnp.bfloat16)
    projection_grad = jnp.stack(
        [
            product_left(attend_in, query_grad),
            product_left(attend_in, key_grad),
            product_left(attend_in, value_grad),
        ]
    )
    bias_grad = jnp.stack(
        [
            jnp.sum(query_grad.astype(jnp.float32), axis=0),
            jnp.sum(value_grad.astype(jnp.float32), axis=0),
        ]
    )
    total = product_right(query_grad, input_projection[0])
    total = total + product_right(key_grad, input_projection[1])
    normed_one_grad = lax.psum_scatter(
        (total + product_right(value_grad, input_projection[2])).astype(jnp.bfloat16),
        "narrow",
        scatter_dimension=0,
        tiled=True,
    ).astype(jnp.float32)
    one_back = jax.vjp(layer_norm, inputs, norm_gains[0], offsets[0])[1](normed_one_grad)
    tokens_grad = mixed_grad + one_back[0]
    summed = (
        lax.psum_scatter(projection_grad, "dp", scatter_dimension=1, tiled=True),
        lax.psum_scatter(output_grad, "dp", scatter_dimension=1, tiled=True),
        lax.psum_scatter(inner_grad, "dp", scatter_dimension=0, tiled=True),
        lax.psum_scatter(outer_grad, "dp", scatter_dimension=1, tiled=True),
        lax.psum_scatter(head_grads[0], "dp", scatter_dimension=1, tiled=True),
        lax.psum_scatter(head_grads[1], "dp", scatter_dimension=0, tiled=True),
        lax.psum_scatter(head_grads[2], "dp", scatter_dimension=1, tiled=True),
        lax.psum_scatter(head_grads[3], "dp", scatter_dimension=0, tiled=True),
        lax.psum_scatter(head_grads[4], "dp", scatter_dimension=0, tiled=True),
        lax.psum_scatter(head_grads[5], "dp", scatter_dimension=0, tiled=True),
    )
    block_sums = summed[:4]
    head_sums = summed[4:]

    def placed(values, axis):
        shape = list(values.shape)
        shape[axis] = values.shape[axis] * narrow_count
        return lax.dynamic_update_slice_in_dim(
            jnp.zeros(shape, jnp.float32), values, narrow_index * values.shape[axis], axis
        )

    bias_whole = placed(bias_grad, 1)
    inner_bias_whole = placed(inner_bias_grad, 0)
    table_whole = placed(table_grad, 1)
    gain_stack = jnp.stack([one_back[1], two_back[1], head_back[1]])
    offset_stack = jnp.stack(
        [one_back[2], attend_bias_grad, two_back[2], outer_bias_grad, head_back[2]]
    )
    small = lax.psum(
        (gain_stack, offset_stack, bias_whole, inner_bias_whole, table_whole), ("dp", "narrow")
    )
    return (
        block_out.astype(jnp.bfloat16),
        logits,
        tokens_grad,
        block_sums[0],
        small[2],
        small[4],
        block_sums[1],
        block_sums[2],
        small[3],
        block_sums[3],
        small[0],
        small[1],
        head_sums[0],
        head_sums[1],
        head_sums[2],
        head_sums[3],
        head_sums[4],
        head_sums[5],
        direction_grad,
        gain_grad,
    )


def solution(mesh):
    placed = (
        P(("dp", "narrow"), None),
        P(None, None, "narrow"),
        P(),
        P(),
        P("narrow", None),
        P(None, "narrow"),
        P(),
        P("narrow", None),
        P(),
        P(),
        P(),
        P(),
        P(),
        P(),
        P(),
        P(),
        P(None, ("dp", "narrow")),
        P(("dp", "narrow")),
        P("dp", None),
        P(("dp", "narrow")),
        P(("dp", "narrow"), None),
        P(None, ("dp", "narrow")),
    )
    return jax.shard_map(
        shards,
        mesh=mesh,
        in_specs=placed,
        out_specs=(
            P(("dp", "narrow"), None),
            P(None, ("dp", "narrow")),
            P(("dp", "narrow"), None),
            P(None, "dp", "narrow"),
            P(),
            P(),
            P("narrow", "dp"),
            P("dp", "narrow"),
            P(),
            P("narrow", "dp"),
            P(),
            P(),
            P(None, "dp"),
            P("dp"),
            P(None, "dp"),
            P("dp"),
            P("dp", None),
            P("dp"),
            P(None, ("dp", "narrow")),
            P(("dp", "narrow")),
        ),
        check_vma=False,
    )
```

profile of v0, /device:TPU:0, one launch (start us, length us, event | category | flops | bytes accessed | tf_op | source)
XLA Modules:
  0.0 1414.3 jit_solution(2788142734849389156)
XLA Ops:
  17.9 37.5 %all-gather.6.cloned.1.call-done = bf16[3136,768]{1,0:T(8,128)(2,1)} async-done(((bf16[784,768]{1,0:T(8,128)(2,1)}), bf16[3136,768]{1,0:T(8,128)(2,1)}) %all-gather.6.cloned.1.call-update) | async-done | bytes 4816912 | tf_op jit(solution)/shard_map/all_gather | solution.py:137
  60.6 11.1 reshape.342
  76.8 11.2 reshape.343
  88.0 15.3 %fusion.6 = (f32[64,6,49]{2,1,0:T(8,128)S(1)}, f32[64,6,49,49]{2,3,1,0:T(8,128)S(1)}) fusion(f32[6,49,49]{1,2,0:T(8,128)S(1)} %copy.113, bf16[64,49,6,32]{1,0,3,2:T(8,128)(2,1)} %reshape.343, bf16[64,49,6,32]{1,0,3,2:T(8,128)(2,1)} %reshape.342), kind=kOutput, calls=%fused_computation.25 | convolution fusion | flops 61754112 | bytes 6229272 | tf_op jit(solution)/shard_map/wihd,wjhd->whij/dot_general | solution.py:162
  113.5 11.0 reshape.341
  124.5 12.5 convert_bitcast_fusion.1
  151.9 48.6 %reduce-scatter.16.cloned.1.call-done = bf16[784,768]{1,0:T(8,128)(2,1)} async-done(((bf16[3136,768]{1,0:T(8,128)(2,1)}), bf16[784,768]{1,0:T(8,128)(2,1)}) %reduce-scatter.16.cloned.1.call-update) | async-done | bytes 1204240 | tf_op jit(solution)/shard_map/reduce_scatter | solution.py:178
  206.1 37.3 %all-gather.8.cloned.1.call-done = bf16[3136,768]{1,0:T(8,128)(2,1)} async-done(((bf16[784,768]{1,0:T(8,128)(2,1)}), bf16[3136,768]{1,0:T(8,128)(2,1)}) %all-gather.8.cloned.1.call-update) | async-done | bytes 4816912 | tf_op jit(solution)/shard_map/all_gather | solution.py:186
  243.5 27.2 %multiply_convert_fusion.1 = (bf16[3136,768]{1,0:T(8,128)(2,1)S(1)}, f32[3136,768]{1,0:T(8,128)}, f32[3136,768]{1,0:T(8,128)}) fusion(f32[768]{0:T(1024)S(1)} %dynamic_slice.14, bf16[3136,768]{1,0:T(8,128)(2,1)} %all-gather.8.cloned.1.call-done, bf16[768,768]{1,0:T(8,128)(2,1)} %param.27), kind=kOutput, calls=%fused_computation.11 | convolution fusion | flops 3858333696 | bytes 30084096 | tf_op jit(solution)/shard_map/dot_general | solution.py:36
  283.4 39.9 %psum.50 = f32[32,256]{1,0:T(8,128)S(1)} all-reduce(f32[32,256]{1,0:T(8,128)S(1)} %convolution_bitcast_fusion.4), channel_id=1, replica_groups=mesh['dp'=8,'narrow'=4] {'dp','narrow'}, use_global_device_ids=true, to_apply=%region_15.16 | all-reduce | flops 8192 | bytes 65536 | tf_op jit(solution)/shard_map/psum | solution.py:226
  333.7 10.1 psum.49
  361.4 39.1 %all-gather.10.cloned.1.call-done = bf16[3136,768]{1,0:T(8,128)(2,1)} async-done(((bf16[784,768]{1,0:T(8,128)(2,1)}), bf16[3136,768]{1,0:T(8,128)(2,1)}) %all-gather.10.cloned.1.call-update) | async-done | bytes 4816912 | tf_op jit(solution)/shard_map/all_gather | solution.py:233
  400.5 13.6 convert_reduce_fusion.1
  422.0 48.6 %reduce-scatter.20.cloned.1.call-done = bf16[784,768]{1,0:T(8,128)(2,1)} async-done(((bf16[3136,768]{1,0:T(8,128)(2,1)}), bf16[784,768]{1,0:T(8,128)(2,1)}) %reduce-scatter.20.cloned.1.call-update) | async-done | bytes 1204240 | tf_op jit(solution)/shard_map/reduce_scatter | solution.py:238
  479.3 38.1 %all-gather.12.cloned.1.call-done = bf16[3136,768]{1,0:T(8,128)(2,1)} async-done(((bf16[784,768]{1,0:T(8,128)(2,1)}), bf16[3136,768]{1,0:T(8,128)(2,1)}) %all-gather.12.cloned.1.call-update) | async-done | bytes 4816912 | tf_op jit(solution)/shard_map/all_gather | solution.py:247
  521.6 10.2 reshape.347
  531.8 14.7 %convert_reduce_fusion.2 = (f32[6,32]{1,0:T(8,128)S(1)}, bf16[64,49,6,32]{1,3,2,0:T(8,128)(2,1)}) fusion(f32[64,6,49,49]{2,3,1,0:T(8,128)} %copy-done.2, f32[64,6,49]{2,1,0:T(8,128)S(1)} %copy-done.23, f32[6,49,49]{1,2,0:T(8,128)S(1)} %copy-done.21, bf16[64,49,6,32]{1,0,3,2:T(8,128)(2,1)} %reshape.347), kind=kOutput, calls=%fused_computation.29 | convolution fusion | flops 64501056 | bytes 6230040 | tf_op jit(solution)/shard_map/whij,wihd->wjhd/dot_general | solution.py:252
  546.4 16.2 %multiply_reduce_fusion = (f32[64,6,49]{2,1,0:T(8,128)S(1)}, f32[64,6,49,49]{2,3,1,0:T(8,128)}) fusion(f32[64,6,49,49]{2,3,1,0:T(8,128)} %copy-done.2, f32[64,6,49]{2,1,0:T(8,128)S(1)} %copy-done.23, f32[6,49,49]{1,2,0:T(8,128)S(1)} %copy-done.21, bf16[64,49,6,32]{1,0,3,2:T(8,128)(2,1)} %reshape.341, bf16[64,49,6,32]{1,0,3,2:T(8,128)(2,1)S(1)} %copy-done.10), kind=kOutput, calls=%fused_computation.3 | convolution fusion | flops 63598080 | bytes 9992472 | tf_op jit(solution)/shard_map/wihd,wjhd->whij/dot_general | solution.py:259
  562.7 9.1 convert_reduce_fusion
  571.8 8.2 fusion.15
  660.1 9.5 fusion.127
  669.7 9.5 fusion.126
  683.1 8.2 fusion.128
  693.8 37.4 %all-reduce.4 = (f32[2048]{0:T(1024)S(1)}, f32[2048]{0:T(1024)S(1)}, f32[256]{0:T(256)S(1)}) all-reduce(f32[2048]{0:T(1024)S(1)} %get-tuple-element.153, f32[2048]{0:T(1024)S(1)} %get-tuple-element.189, f32[256]{0:T(256)S(1)} %get-tuple-element.151), channel_id=11, replica_groups=mesh['dp'=8,'narrow'=4] {'dp'}, use_global_device_ids=true, to_apply=%region_49.50.clone | all-reduce | flops 4352 | bytes 34816
  732.5 26.3 %all-gather = bf16[8,4,256]{2,1,0:T(4,128)(2,1)S(1)} all-gather(bf16[1,4,256]{2,1,0:T(4,128)(2,1)S(1)} %get-tuple-element.174), channel_id=1, replica_groups=mesh['dp'=8,'narrow'=4] {'dp'}, dimensions={0}, use_global_device_ids=true | all-gather | bytes 18432 | tf_op jit(solution)/shard_map/all_gather | solution.py:209
  769.1 14.1 reduce-scatter.22.cloned.1.call-done
  787.0 42.3 %all-reduce.3 = (f32[2,768]{1,0:T(2,128)}, f32[169,24]{0,1:T(8,128)}, f32[3072]{0:T(1024)}, f32[3,768]{1,0:T(4,128)}, f32[5,768]{1,0:T(8,128)}) all-reduce(f32[2,768]{1,0:T(2,128)S(1)} %dynamic_update_slice.9, f32[169,24]{0,1:T(8,128)S(1)} %dynamic_update_slice.10, ...), channel_id=1, replica_groups=mesh['dp'=8,'narrow'=4] {'dp','narrow'}, use_global_device_ids=true, to_apply=%region_29.30 | all-reduce | flops 14808 | bytes 118464 | tf_op jit(solution)/shard_map/psum | solution.py:333
  833.4 22.1 %reduce-scatter.32.cloned.1.call-done = f32[256,256]{1,0:T(8,128)} async-done(((f32[2048,256]{1,0:T(8,128)}), f32[256,256]{1,0:T(8,128)}) %reduce-scatter.32.cloned.1.call-update) | async-done | bytes 262160 | tf_op jit(solution)/shard_map/reduce_scatter | solution.py:313
  855.5 72.0 %reduce-scatter.26.cloned.1.call-done = f32[768,96]{0,1:T(8,128)} async-done(((f32[768,768]{0,1:T(8,128)}), f32[768,96]{0,1:T(8,128)}) %reduce-scatter.26.cloned.1.call-update) | async-done | bytes 294928 | tf_op jit(solution)/shard_map/reduce_scatter | solution.py:308
  927.5 72.3 %reduce-scatter.24.cloned.1.call-done = f32[96,768]{1,0:T(8,128)} async-done(((f32[768,768]{1,0:T(8,128)}), f32[96,768]{1,0:T(8,128)}) %reduce-scatter.24.cloned.1.call-update) | async-done | bytes 294928 | tf_op jit(solution)/shard_map/reduce_scatter | solution.py:307
  999.8 121.5 %reduce-scatter.28.cloned.1.call-done = f32[768,256]{1,0:T(8,128)} async-done(((f32[768,2048]{1,0:T(8,128)}), f32[768,256]{1,0:T(8,128)}) %reduce-scatter.28.cloned.1.call-update) | async-done | bytes 786448 | tf_op jit(solution)/shard_map/reduce_scatter | solution.py:309
  1121.3 286.0 %reduce-scatter.30.cloned.1.call-done = f32[2048,256]{1,0:T(8,128)} async-done(((f32[2048,2048]{1,0:T(8,128)}), f32[2048,256]{1,0:T(8,128)}) %reduce-scatter.30.cloned.1.call-update) | async-done | bytes 2097168 | tf_op jit(solution)/shard_map/reduce_scatter | solution.py:311
  (290 shorter events, 217.2 us)
Async XLA Ops:
  7.2 336.6 %copy-start = (bf16[768,2048]{1,0:T(8,128)(2,1)S(1)}, bf16[768,2048]{1,0:T(8,128)(2,1)}, u32[]{:S(2)}) copy-start(bf16[768,2048]{1,0:T(8,128)(2,1)} %param.32) | copy-start | bytes 9437188
  7.2 48.2 %all-gather.6.cloned.1.call-start = ((), (), s32[]{:S(2)}) async-start(), calls=%async_computation.11 | async-start | bytes 6021120 | tf_op jit(solution)/shard_map/all_gather | solution.py:137
  14.5 186.0 %reduce-scatter.16.cloned.1.call-start = ((), (), s32[]{:S(2)}) async-start(), calls=%async_computation.12 | async-start | bytes 6021120 | tf_op jit(solution)/shard_map/reduce_scatter | solution.py:178
  17.1 107.4 %copy-start.20 = (f32[6,49,49]{1,2,0:T(8,128)}, f32[6,49,49]{1,2,0:T(8,128)S(1)}, u32[]{:S(2)}) copy-start(f32[6,49,49]{1,2,0:T(8,128)S(1)} %copy.113) | copy-start | bytes 172876
  151.8 91.6 %all-gather.8.cloned.1.call-start = ((), (), s32[]{:S(2)}) async-start(), calls=%async_computation.13 | async-start | bytes 6021120 | tf_op jit(solution)/shard_map/all_gather | solution.py:186
  205.3 122.6 %reduce-scatter.18.cloned.1.call-start = ((), (), s32[]{:S(2)}) async-start(), calls=%async_computation.14 | async-start | bytes 6021120 | tf_op jit(solution)/shard_map/reduce_scatter | solution.py:189
  243.5 29.5 %copy-start.55 = (bf16[768,768]{1,0:T(8,128)(2,1)S(1)}, bf16[768,768]{1,0:T(8,128)(2,1)}, u32[]{:S(2)}) copy-start(bf16[768,768]{1,0:T(8,128)(2,1)} %param.29) | copy-start | bytes 3538948
  278.6 122.0 %all-gather.10.cloned.1.call-start = ((), (), s32[]{:S(2)}) async-start(), calls=%async_computation.15 | async-start | bytes 6021120 | tf_op jit(solution)/shard_map/all_gather | solution.py:233
  281.1 49.5 %copy-start.40 = (f32[2048]{0:T(1024)}, f32[2048]{0:T(1024)S(1)}, u32[]{:S(2)}) copy-start(f32[2048]{0:T(1024)S(1)} %fusion.61) | copy-start | bytes 24580
  361.4 109.3 %reduce-scatter.20.cloned.1.call-start = ((), (), s32[]{:S(2)}) async-start(), calls=%async_computation.16 | async-start | bytes 6021120 | tf_op jit(solution)/shard_map/reduce_scatter | solution.py:238
  422.0 48.7 %copy-start.5 = (bf16[784,768]{1,0:T(8,128)(2,1)S(1)}, bf16[784,768]{1,0:T(8,128)(2,1)}, u32[]{:S(2)}) copy-start(bf16[784,768]{1,0:T(8,128)(2,1)} %param.22) | copy-start | bytes 3612676
  422.0 48.7 %copy-start.9 = (bf16[784,768]{1,0:T(8,128)(2,1)S(1)}, bf16[784,768]{1,0:T(8,128)(2,1)}, u32[]{:S(2)}) copy-start(bf16[784,768]{1,0:T(8,128)(2,1)} %reduce-scatter.16.cloned.1.call-done) | copy-start | bytes 3612676
  422.0 95.4 %all-gather.12.cloned.1.call-start = ((), (), s32[]{:S(2)}) async-start(), calls=%async_computation.17 | async-start | bytes 6021120 | tf_op jit(solution)/shard_map/all_gather | solution.py:247
  476.7 40.8 %copy-start.35 = (bf16[192,768]{1,0:T(8,128)(2,1)S(1)}, bf16[192,768]{1,0:T(8,128)(2,1)}, u32[]{:S(2)}) copy-start(bf16[192,768]{1,0:T(8,128)(2,1)} %param.26) | copy-start | bytes 884740
  479.3 286.3 %reduce-scatter.36.cloned.1.call-start = ((), (), s32[]{:S(2)}) async-start(), calls=%async_computation.25 | async-start | bytes 884736
  601.2 166.0 %reduce-scatter.34.cloned.1.call-start = ((), (), s32[]{:S(2)}) async-start(), calls=%async_computation.24 | async-start | bytes 2211840
  642.3 140.9 %reduce-scatter.22.cloned.1.call-start = ((), (), s32[]{:S(2)}) async-start(), calls=%async_computation.18 | async-start | bytes 6021120 | tf_op jit(solution)/shard_map/reduce_scatter | solution.py:296
  658.0 197.6 %reduce-scatter.32.cloned.1.call-start = ((), (), s32[]{:S(2)}) async-start(), calls=%async_computation.23 | async-start | bytes 2359296 | tf_op jit(solution)/shard_map/reduce_scatter | solution.py:313
  660.1 267.4 %reduce-scatter.26.cloned.1.call-start = ((), (), s32[]{:S(2)}) async-start(), calls=%async_computation.20 | async-start | bytes 2654208 | tf_op jit(solution)/shard_map/reduce_scatter | solution.py:308
  669.7 330.1 %reduce-scatter.24.cloned.1.call-start = ((), (), s32[]{:S(2)}) async-start(), calls=%async_computation.19 | async-start | bytes 2654208 | tf_op jit(solution)/shard_map/reduce_scatter | solution.py:307
  679.2 442.1 %reduce-scatter.28.cloned.1.call-start = ((), (), s32[]{:S(2)}) async-start(), calls=%async_computation.21 | async-start | bytes 7077888 | tf_op jit(solution)/shard_map/reduce_scatter | solution.py:309
  683.0 724.3 %reduce-scatter.30.cloned.1.call-start = ((), (), s32[]{:S(2)}) async-start(), calls=%async_computation.22 | async-start | bytes 18874368 | tf_op jit(solution)/shard_map/reduce_scatter | solution.py:311
  691.3 68.1 %copy-start.31 = (bf16[256,2048]{1,0:T(8,128)(2,1)S(1)}, bf16[256,2048]{1,0:T(8,128)(2,1)}, u32[]{:S(2)}) copy-start(bf16[256,2048]{1,0:T(8,128)(2,1)} %param.38) | copy-start | bytes 3145732
  691.3 68.1 %copy-start.47 = (f32[2048]{0:T(1024)S(1)}, f32[2048]{0:T(1024)}, u32[]{:S(2)}) copy-start(f32[2048]{0:T(1024)} %copy-done.46) | copy-start | bytes 24580
  691.3 68.1 %copy-start.54 = (f32[2048]{0:T(1024)S(1)}, f32[2048]{0:T(1024)}, u32[]{:S(2)}) copy-start(f32[2048]{0:T(1024)} %param.39) | copy-start | bytes 24580
  691.3 68.1 %copy-start.58 = (bf16[32,2048]{1,0:T(8,128)(2,1)S(1)}, bf16[32,2048]{1,0:T(8,128)(2,1)}, u32[]{:S(2)}) copy-start(bf16[32,2048]{1,0:T(8,128)(2,1)} %param.43) | copy-start | bytes 393220
  691.3 68.7 %copy-start.41 = (f32[2048]{0:T(1024)S(1)}, f32[2048]{0:T(1024)}, u32[]{:S(2)}) copy-start(f32[2048]{0:T(1024)} %copy-done.40) | copy-start | bytes 24580
  763.6 19.6 %copy-start.37 = (f32[784]{0:T(1024)S(1)}, f32[784]{0:T(1024)}, u32[]{:S(2)}) copy-start(f32[784]{0:T(1024)} %copy-done.36) | copy-start | bytes 9412
  763.6 19.6 %copy-start.39 = (f32[768]{0:T(1024)S(1)}, f32[768]{0:T(1024)}, u32[]{:S(2)}) copy-start(f32[768]{0:T(1024)} %copy-done.38) | copy-start | bytes 9220
  764.2 21.3 %copy-start.45 = (f32[784]{0:T(1024)S(1)}, f32[784]{0:T(1024)}, u32[]{:S(2)}) copy-start(f32[784]{0:T(1024)} %copy-done.44) | copy-start | bytes 9412
  764.2 21.3 %copy-start.43 = (f32[784]{0:T(1024)S(1)}, f32[784]{0:T(1024)}, u32[]{:S(2)}) copy-start(f32[784]{0:T(1024)} %copy-done.42) | copy-start | bytes 9412
  829.4 578.0 %copy-start.1 = (bf16[768,2048]{1,0:T(8,128)(2,1)S(1)}, bf16[768,2048]{1,0:T(8,128)(2,1)}, u32[]{:S(2)}) copy-start(bf16[768,2048]{1,0:T(8,128)(2,1)} %param.32) | copy-start | bytes 9437188
  (49 other events, 227.4 us)
Sparse Core Ops, SparseCore 0:
  14.6 40.6 all-gather.5
  152.0 48.4 reduce-scatter.15
  205.4 38.0 all-gather.7
  278.7 49.1 reduce-scatter.17
  361.5 39.0 all-gather.9
  422.1 48.4 reduce-scatter.19
  479.4 38.0 all-gather.11
  601.3 62.5 reduce-scatter.35
  667.4 65.7 reduce-scatter.33
  735.8 47.3 reduce-scatter.21
  787.3 68.1 reduce-scatter.31
  859.5 67.9 reduce-scatter.25
  931.6 68.1 reduce-scatter.23
  1003.8 117.4 reduce-scatter.27
  1125.5 281.7 reduce-scatter.29
where the time goes:
time: 1420 us; the launch traced here: 1410 us
  waiting for transfers between devices  842 us (59%)
  matrix products  236 us (17%)
  blocking collectives  156 us (11%)
  local copies, waits for them, and re-layouts  113 us (8%)
  other arithmetic  49.8 us (4%)
  between operations  16.6 us (1%)
    reduce_scatter x1, waiting for transfers between devices, shards(): lax.psum_scatter(head_grads[2], 'dp', scatter_dimension=1, tiled=True)  286 us
    reduce_scatter x1, waiting for transfers between devices, shards(): lax.psum_scatter(head_grads[0], 'dp', scatter_dimension=1, tiled=True)  122 us
    reduce_scatter x1, waiting for transfers between devices, shards(): lax.psum_scatter(inner_grad, 'dp', scatter_dimension=0, tiled=True)  72.3 us
    reduce_scatter x1, waiting for transfers between devices, shards(): lax.psum_scatter(outer_grad, 'dp', scatter_dimension=1, tiled=True)  72 us
    dot_general x10, matrix products, product(): return jnp.dot(left, right, preferred_element_type=jnp.float32)  60.2 us
    reduce_scatter x1, waiting for transfers between devices, shards(): lax.psum_scatter(product(attended, output_projection).astype(jnp.bfloat16...  48.6 us
    reduce_scatter x1, waiting for transfers between devices, shards(): lax.psum_scatter(product_right(pre_grad, inner_weight).astype(jnp.bfloat1...  48.6 us
    dot_general x9, matrix products, product_left(): lax.dot_general(left, right, (((0,), (0,)), ((), ())), preferred_element_...  45.6 us
  transfers between devices with their start and end apart: 15, of which 13 were waited for; matrix products, arithmetic and copies ran while one was open for 8% of the time, Pallas kernels for 0%

commit v1 on v0

v1 whole, which is shorter than its diff:
```python
import functools

import jax
import jax.numpy as jnp
from jax import lax
from jax.experimental import pallas as pl
from jax.experimental.pallas import tpu as pltpu
from jax.sharding import PartitionSpec as P

HIGH = lax.Precision.HIGHEST
F32 = jnp.float32
BF16 = jnp.bfloat16
SIDE = 7
SPOTS = SIDE * SIDE
PAD = 64
VMEM_LIMIT = 60 * 1024 * 1024
NEG = -1e30


def dot(left, right):
    return jnp.dot(left, right, preferred_element_type=F32)


def dot_left(left, right):
    return lax.dot_general(left, right, (((0,), (0,)), ((), ())), preferred_element_type=F32)


def dot_right(left, right):
    return lax.dot_general(left, right, (((1,), (1,)), ((), ())), preferred_element_type=F32)


def call(body, outs, ins, **kw):
    scratch = kw.pop("scratch", ())
    return pl.pallas_call(
        body,
        out_shape=outs,
        in_specs=[pl.BlockSpec(memory_space=pltpu.VMEM)] * len(ins),
        out_specs=jax.tree.map(lambda _: pl.BlockSpec(memory_space=pltpu.VMEM), outs),
        scratch_shapes=scratch,
        compiler_params=pltpu.CompilerParams(vmem_limit_bytes=VMEM_LIMIT),
        **kw,
    )(*ins)


def shape(dims, kind):
    return jax.ShapeDtypeStruct(dims, kind)


def norm_parts(values):
    center = values - jnp.mean(values, axis=-1, keepdims=True)
    spread = jnp.mean(center * center, axis=-1, keepdims=True)
    inv = lax.rsqrt(spread + 1e-05)
    return center * inv, inv


def norm_back(nhat, inv, gain, grad):
    scaled = grad * gain
    first = jnp.mean(scaled, axis=-1, keepdims=True)
    second = jnp.mean(scaled * nhat, axis=-1, keepdims=True)
    return (scaled - first - nhat * second) * inv


def gelu_pair(pre):
    bell = jnp.exp(pre * pre * -0.5)
    dist = jnp.abs(pre) * (0.3275911 * 0.70710678118654752) + 1.0
    inv = 1.0 / dist
    poly = 0.5 * 1.061405429
    for coef in (-1.453152027, 1.421413741, -0.284496736, 0.254829592):
        poly = poly * inv + 0.5 * coef
    tail = poly * inv * bell
    cdf = jnp.where(pre < 0.0, tail, 1.0 - tail)
    return pre * cdf, cdf + pre * (bell * 0.3989422804014327)


def norm_one_body(windows, tokens, gain, shift, padded, flat):
    rows = tokens.shape[0]
    step = 112
    for r in range(0, rows, step):
        nhat, _ = norm_parts(tokens[r : r + step, :].astype(F32))
        flat[r : r + step, :] = nhat * gain[...] + shift[...]
    place = lax.broadcasted_iota(jnp.int32, (PAD, 1), 0)
    for w in range(windows):
        block = flat[w * SPOTS : w * SPOTS + PAD, :]
        padded[w * PAD : (w + 1) * PAD, :] = jnp.where(place < SPOTS, block, 0.0).astype(BF16)


def head_masks(heads, size):
    lane = lax.broadcasted_iota(jnp.int32, (PAD, heads * size), 1) // size
    return [lane == h for h in range(heads)]


def spread_heads(values, masks):
    zero = jnp.zeros_like(values)
    return jnp.concatenate([jnp.where(m, values, zero) for m in masks], axis=0)


def fold_heads(values, masks):
    total = values[0:PAD, :]
    for h in range(1, len(masks)):
        total = jnp.where(masks[h], values[h * PAD : (h + 1) * PAD, :], total)
    return total


def attend_body(heads, scale, padded, weight, bias, table, q_out, k_out, v_out, p_out, att_out):
    rows, width = q_out.shape
    size = width // heads
    x = padded[...]
    q_out[...] = (dot(x, weight[0]) + bias[0:1, :]).astype(BF16)
    k_out[...] = dot(x, weight[1]).astype(BF16)
    v_out[...] = (dot(x, weight[2]) + bias[1:2, :]).astype(BF16)
    masks = head_masks(heads, size)

    def window(w, carry):
        here = pl.ds(pl.multiple_of(w * PAD, PAD), PAD)
        spread = spread_heads(q_out[here, :], masks)
        scores = dot_right(k_out[here, :], spread) * scale + table[...]
        top = jnp.max(scores, axis=0, keepdims=True)
        e = jnp.exp(scores - top)
        probs = (e * (1.0 / jnp.sum(e, axis=0, keepdims=True))).astype(BF16)
        p_out[here, :] = probs
        att_out[here, :] = fold_heads(dot_left(probs, v_out[here, :]), masks).astype(BF16)
        return carry

    lax.fori_loop(0, rows // PAD, window, 0, unroll=4)


def attend_back_body(
    heads, scale, low, weight, q_in, k_in, v_in, p_in, d_out, table_out, sums_out, given
):
    rows, width = q_in.shape
    size = width // heads
    given[...] = dot_right(low[...], weight[...]).astype(BF16)
    masks = head_masks(heads, size)
    table_out[...] = jnp.zeros_like(table_out)

    def window(w, carry):
        here = pl.ds(pl.multiple_of(w * PAD, PAD), PAD)
        qs = spread_heads(q_in[here, :], masks)
        gs = spread_heads(given[here, :], masks)
        probs_low = p_in[here, :]
        probs = probs_low.astype(F32)
        prob_grad = dot_right(v_in[here, :], gs)
        mean = jnp.sum(probs * prob_grad, axis=0, keepdims=True)
        score_low = (probs * (prob_grad - mean)).astype(BF16)
        table_out[...] += score_low.astype(F32)
        dq = (fold_heads(dot_left(score_low, k_in[here, :]), masks) * scale).astype(BF16)
        dk = (dot(score_low, qs) * scale).astype(BF16)
        dv = dot(probs_low, gs).astype(BF16)
        d_out[here, 0:width] = dq
        d_out[here, width : 2 * width] = dk
        d_out[here, 2 * width : 3 * width] = dv
        return carry

    lax.fori_loop(0, rows // PAD, window, 0, unroll=4)
    sums_out[...] = jnp.sum(d_out[...].astype(F32), axis=0, keepdims=True)


def mixed_body(windows, count, *refs):
    att, wo = refs[:count], refs[count : 2 * count]
    tokens, vecs, mixed, normed = refs[2 * count :]
    for w in range(windows):
        here = slice(w * PAD, (w + 1) * PAD)
        total = dot(att[0][here, :], wo[0][...])
        for k in range(1, count):
            total = total + dot(att[k][here, :], wo[k][...])
        mixed[w * SPOTS : (w + 1) * SPOTS, :] = total[0:SPOTS, :]
    step = 112
    for r in range(0, tokens.shape[0], step):
        rows = slice(r, r + step)
        value = tokens[rows, :].astype(F32) + mixed[rows, :] + vecs[0:1, :]
        mixed[rows, :] = value
        nhat, _ = norm_parts(value)
        normed[rows, :] = (nhat * vecs[1:2, :] + vecs[2:3, :]).astype(BF16)


def inner_body(blocks, count, *refs):
    normed, mixed, bias = refs[:3]
    wi, wo = refs[3 : 3 + count], refs[3 + count : 3 + 2 * count]
    vecs, crop, act_out, slope_out, block_out, features, pool, total = refs[3 + 2 * count :]
    step = pl.program_id(0)

    @pl.when(step == 0)
    def _():
        total[...] = jnp.zeros_like(total)

    for k in range(count):

        @pl.when(step // blocks == k)
        def _(k=k):
            pre = dot(normed[...], wi[k][...]) + bias[0]
            act, slope = gelu_pair(pre)
            act = act.astype(BF16)
            act_out[...] = act
            slope_out[...] = slope.astype(BF16)
            total[...] += dot(act, wo[k][...])

    @pl.when(step == blocks * count - 1)
    def _():
        crops = pool.shape[0]
        sums = [jnp.zeros((1, total.shape[1]), F32)] * crops
        rows_step = 112
        for r in range(0, total.shape[0], rows_step):
            rows = slice(r, r + rows_step)
            value = mixed[rows, :] + total[rows, :] + vecs[0:1, :]
            block_out[rows, :] = value
            features[rows, :] = value.astype(BF16)
            nhat, _ = norm_parts(value)
            head = nhat * vecs[1:2, :] + vecs[2:3, :]
            for c in range(crops):
                sums[c] = sums[c] + jnp.sum(
                    jnp.where(crop[rows, :] == c, head, 0.0), axis=0, keepdims=True
                )
        for c in range(crops):
            pool[c : c + 1, :] = sums[c]


def head_back_body(block_out, cotangent, crop, pooled_grad, gain, grad_out, low_out, sums_out):
    crops = pooled_grad.shape[0]
    step = 112
    gain_sum = jnp.zeros((1, block_out.shape[1]), F32)
    shift_sum = gain_sum
    bias_sum = gain_sum
    for r in range(0, block_out.shape[0], step):
        rows = slice(r, r + step)
        nhat, inv = norm_parts(block_out[rows, :])
        grad = jnp.zeros(nhat.shape, F32)
        for c in range(crops):
            grad = jnp.where(crop[rows, :] == c, pooled_grad[c : c + 1, :], grad)
        gain_sum = gain_sum + jnp.sum(grad * nhat, axis=0, keepdims=True)
        shift_sum = shift_sum + jnp.sum(grad, axis=0, keepdims=True)
        out = cotangent[rows, :].astype(F32) + norm_back(nhat, inv, gain[...], grad)
        bias_sum = bias_sum + jnp.sum(out, axis=0, keepdims=True)
        grad_out[rows, :] = out
        low_out[rows, :] = out.astype(BF16)
    sums_out[0:1, :] = gain_sum
    sums_out[1:2, :] = shift_sum
    sums_out[2:3, :] = bias_sum


def mixed_back_body(windows, mixed, out_grad, normed_grad, gain, grad_out, low_out, sums_out, flat):
    rows_all = mixed.shape[0]
    step = 112
    gain_sum = jnp.zeros((1, mixed.shape[1]), F32)
    shift_sum = gain_sum
    bias_sum = gain_sum
    for r in range(0, rows_all, step):
        rows = slice(r, r + step)
        nhat, inv = norm_parts(mixed[rows, :])
        grad = normed_grad[rows, :]
        gain_sum = gain_sum + jnp.sum(grad * nhat, axis=0, keepdims=True)
        shift_sum = shift_sum + jnp.sum(grad, axis=0, keepdims=True)
        out = out_grad[rows, :] + norm_back(nhat, inv, gain[...], grad)
        bias_sum = bias_sum + jnp.sum(out, axis=0, keepdims=True)
        grad_out[rows, :] = out
        flat[rows, :] = out
    sums_out[0:1, :] = gain_sum
    sums_out[1:2, :] = shift_sum
    sums_out[2:3, :] = bias_sum
    place = lax.broadcasted_iota(jnp.int32, (PAD, 1), 0)
    for w in range(windows):
        block = flat[w * SPOTS : w * SPOTS + PAD, :]
        low_out[w * PAD : (w + 1) * PAD, :] = jnp.where(place < SPOTS, block, 0.0).astype(BF16)


def tokens_back_body(windows, count, *refs):
    grads, weights = refs[:count], refs[count : 2 * count]
    tokens, mixed_grad, gain, grad_out, sums_out, flat = refs[2 * count :]
    width = weights[0].shape[2]
    for w in range(windows):
        here = slice(w * PAD, (w + 1) * PAD)
        total = jnp.zeros((PAD, tokens.shape[1]), F32)
        for k in range(count):
            for part in range(3):
                total = total + dot_right(
                    grads[k][here, part * width : (part + 1) * width], weights[k][part]
                )
        flat[w * SPOTS : (w + 1) * SPOTS, :] = total[0:SPOTS, :]
    step = 112
    gain_sum = jnp.zeros((1, tokens.shape[1]), F32)
    shift_sum = gain_sum
    for r in range(0, tokens.shape[0], step):
        rows = slice(r, r + step)
        nhat, inv = norm_parts(tokens[rows, :].astype(F32))
        grad = flat[rows, :]
        gain_sum = gain_sum + jnp.sum(grad * nhat, axis=0, keepdims=True)
        shift_sum = shift_sum + jnp.sum(grad, axis=0, keepdims=True)
        grad_out[rows, :] = mixed_grad[rows, :] + norm_back(nhat, inv, gain[...], grad)
    sums_out[0:1, :] = gain_sum
    sums_out[1:2, :] = shift_sum


def swap(values, axis, bit):
    return lax.ppermute(values, axis, [(i, i ^ bit) for i in range(lax.axis_size(axis))])


def bits_of(axis):
    size = lax.axis_size(axis)
    bit, found = 1, []
    while bit < size:
        found.append(bit)
        bit *= 2
    return found


def has_bit(axis, bit):
    return (lax.axis_index(axis) // bit) % 2 == 1


def sum_over(values, axes):
    for axis in axes:
        for bit in bits_of(axis):
            values = values + swap(values, axis, bit)
    return values


def gather_over(values, axis):
    for bit in bits_of(axis):
        other = swap(values, axis, bit)
        upper = has_bit(axis, bit)
        values = jnp.concatenate(
            [jnp.where(upper, other, values), jnp.where(upper, values, other)], axis=0
        )
    return values


def by_distance(values, axis):
    for bit in bits_of(axis):
        size = values.shape[0]
        folded = values.reshape(size // (2 * bit), 2, bit, *values.shape[1:])
        folded = jnp.where(has_bit(axis, bit), folded[:, ::-1], folded)
        values = folded.reshape(values.shape)
    return values


def gathered(weight):
    found = [weight]
    for bit in bits_of("narrow"):
        found = found + [swap(w, "narrow", bit) for w in found]
    return found


def halve_rows(values, bit, low):
    groups, rows, columns = values.shape
    folded = values.reshape(groups // 2, 2, rows, columns)
    mine = lax.axis_index("dp") // bit % 2
    keep = lax.dynamic_index_in_dim(folded, mine, 1, keepdims=False)
    send = lax.dynamic_index_in_dim(folded, 1 - mine, 1, keepdims=False).astype(low)
    return keep, send


def scatter_sum(parts, row_first):
    groups = lax.axis_size("dp")
    parts = [p.reshape(groups, p.shape[0] // groups, p.shape[1]) for p in parts]
    narrow_bits = bits_of("narrow")
    dp_bits = bits_of("dp")

    def over_narrow(parts, bit):
        kept = [p for k, p in enumerate(parts) if not k & bit]
        sent = [p for k, p in enumerate(parts) if k & bit]
        return [a.astype(F32) + swap(b.astype(BF16), "narrow", bit).astype(F32) for a, b in zip(kept, sent)]

    def over_dp(parts, bit):
        done = []
        for p in parts:
            keep, send = halve_rows(p, bit, BF16)
            done.append(keep.astype(F32) + swap(send, "dp", bit).astype(F32))
        return done

    parts = [p for p in parts]
    def drop(parts):
        kept = parts[0::2]
        sent = parts[1::2]
        return kept, sent

    steps = [("narrow", b) for b in narrow_bits] + [("dp", b) for b in dp_bits]
    if row_first:
        steps = (
            [("narrow", narrow_bits[0]), ("dp", dp_bits[0])]
            + [("narrow", b) for b in narrow_bits[1:]]
            + [("dp", b) for b in dp_bits[1:]]
        )
    for axis, bit in steps:
        if axis == "narrow":
            kept, sent = drop(parts)
            parts = [
                a.astype(F32) + swap(b.astype(BF16), "narrow", bit).astype(F32)
                for a, b in zip(kept, sent)
            ]
        else:
            parts = over_dp(parts, bit)
    return parts[0].reshape(parts[0].shape[1:])


def gelu_exact(values):
    return jax.nn.gelu(values, approximate=False)


def gelu_back(pre, cotangent):
    return jax.vjp(gelu_exact, pre)[1](cotangent)[0]


def normalize_rows(values):
    return values * lax.rsqrt(jnp.sum(values * values, axis=-1, keepdims=True) + 1e-06)


def offset_table():
    places = jnp.arange(PAD, dtype=jnp.int32)
    row_of = places // SIDE
    col_of = places % SIDE
    offset = (row_of[None, :] - row_of[:, None] + SIDE - 1) * (2 * SIDE - 1) + (
        col_of[None, :] - col_of[:, None] + SIDE - 1
    )
    inside = (places[:, None] < SPOTS) & (places[None, :] < SPOTS)
    offset = jnp.where(inside, offset, -1)
    entries = jnp.arange((2 * SIDE - 1) ** 2, dtype=jnp.int32)
    return (offset.reshape(-1)[:, None] == entries[None, :]).astype(F32)


def shards(
    tokens,
    input_projection,
    input_bias,
    position_bias,
    output_projection,
    inner_weight,
    inner_bias,
    outer_weight,
    norm_gains,
    offsets,
    head_first,
    head_first_bias,
    head_second,
    head_second_bias,
    head_third,
    head_third_bias,
    prototype_direction,
    prototype_gain,
    crop_windows,
    first_epoch,
    feature_cotangent,
    logit_cotangent,
):
    rows, width = tokens.shape
    windows = rows // SPOTS
    narrow_index = lax.axis_index("narrow")
    dp_index = lax.axis_index("dp")
    count = lax.axis_size("narrow")
    groups = lax.axis_size("dp")
    quarter = input_projection.shape[2]
    hidden = inner_weight.shape[1]
    heads = position_bias.shape[1] // count
    size = quarter // heads
    scale = size ** (-0.5)
    crops = crop_windows.shape[1]
    padded_rows = windows * PAD

    w_in = gathered(input_projection)
    w_att = gathered(output_projection)
    w_inner = gathered(inner_weight)
    w_outer = gathered(outer_weight)

    direction = prototype_direction.astype(F32)
    column_inv = lax.rsqrt(jnp.sum(direction * direction, axis=0, keepdims=True) + 1e-06)
    columns_low = (prototype_gain * direction * column_inv).astype(BF16)
    unit_grad = sum_over(dot_right(logit_cotangent, columns_low), ("narrow", "dp"))

    bias_in = by_distance(input_bias.reshape(2, count, quarter).swapaxes(0, 1), "narrow")
    bias_inner = by_distance(inner_bias.reshape(count, 1, hidden), "narrow")
    table = offset_table()
    spread = jnp.dot(table, position_bias, precision=HIGH, preferred_element_type=F32)
    spread = spread.reshape(PAD, PAD, count, heads).transpose(2, 0, 3, 1)
    inside = (jnp.arange(PAD) < SPOTS)[None, :, None, None]
    spread = jnp.where(inside, spread, NEG).reshape(count, PAD, heads * PAD)
    spread = by_distance(spread, "narrow")

    ends = jnp.cumsum(crop_windows[0])
    row_window = narrow_index * windows + jnp.arange(rows, dtype=jnp.int32) // SPOTS
    crop_of_row = jnp.sum((row_window[:, None] >= ends[None, :]).astype(jnp.int32), axis=1, keepdims=True)
    crop_tokens = (crop_windows[0] * SPOTS).astype(F32)

    gains = norm_gains.reshape(3, 1, width)
    padded = call(
        functools.partial(norm_one_body, windows),
        shape((padded_rows, width), BF16),
        (tokens, norm_gains[0:1], offsets[0:1]),
        scratch=[pltpu.VMEM((rows + 16, width), F32)],
    )
    q, k_, v, probs, attended = [], [], [], [], []
    for k in range(count):
        got = call(
            functools.partial(attend_body, heads, scale),
            (
                shape((padded_rows, quarter), BF16),
                shape((padded_rows, quarter), BF16),
                shape((padded_rows, quarter), BF16),
                shape((padded_rows, heads * PAD), BF16),
                shape((padded_rows, quarter), BF16),
            ),
            (padded, w_in[k], bias_in[k], spread[k]),
        )
        for keep, value in zip((q, k_, v, probs, attended), got):
            keep.append(value)
    mixed, normed_two = call(
        functools.partial(mixed_body, windows, count),
        (shape((rows, width), F32), shape((rows, width), BF16)),
        (*attended, *w_att, tokens, jnp.concatenate([offsets[1:2], norm_gains[1:2], offsets[2:3]])),
    )
    blocks = 3
    block = hidden // blocks
    steps = blocks * count

    def block_at(k, column):
        def index(s):
            b = jnp.clip(s - k * blocks, 0, blocks - 1)
            return (0, b) if column else (b, 0)

        return index

    whole = lambda s: (0, 0)
    act, slope, block_out, features, pool = pl.pallas_call(
        functools.partial(inner_body, blocks, count),
        grid=(steps,),
        out_shape=(
            shape((rows, hidden * count), BF16),
            shape((rows, hidden * count), BF16),
            shape((rows, width), F32),
            shape((rows, width), BF16),
            shape((crops, width), F32),
        ),
        in_specs=[
            pl.BlockSpec((rows, width), whole),
            pl.BlockSpec((rows, width), whole),
            pl.BlockSpec((1, 1, block), lambda s: (s // blocks, 0, s % blocks)),
            *[pl.BlockSpec((width, block), block_at(k, True)) for k in range(count)],
            *[pl.BlockSpec((block, width), block_at(k, False)) for k in range(count)],
            pl.BlockSpec((3, width), whole),
            pl.BlockSpec((rows, 1), whole),
        ],
        out_specs=(
            pl.BlockSpec((rows, block), lambda s: (0, s)),
            pl.BlockSpec((rows, block), lambda s: (0, s)),
            pl.BlockSpec((rows, width), whole),
            pl.BlockSpec((rows, width), whole),
            pl.BlockSpec((crops, width), whole),
        ),
        scratch_shapes=[pltpu.VMEM((rows, width), F32)],
        compiler_params=pltpu.CompilerParams(vmem_limit_bytes=VMEM_LIMIT),
    )(
        normed_two,
        mixed,
        bias_inner,
        *w_inner,
        *w_outer,
        jnp.concatenate([offsets[3:4], norm_gains[2:3], offsets[4:5]]),
        crop_of_row,
    )

    pooled_own = (sum_over(pool, ("narrow",)) / crop_tokens[:, None]).astype(BF16)
    pooled = gather_over(pooled_own, "dp")
    first_pre = dot(pooled, head_first) + head_first_bias
    first_act = gelu_exact(first_pre).astype(BF16)
    second_pre = dot(first_act, head_second) + head_second_bias
    second_act = gelu_exact(second_pre).astype(BF16)
    embedded = dot(second_act, head_third) + head_third_bias
    units = normalize_rows(embedded).astype(BF16)
    embed_grad = jax.vjp(normalize_rows, embedded)[1](unit_grad)[0]
    embed_low = embed_grad.astype(BF16)
    second_low = gelu_back(second_pre, dot_right(embed_low, head_third)).astype(BF16)
    first_low = gelu_back(first_pre, dot_right(second_low, head_second)).astype(BF16)
    own_low = lax.dynamic_slice_in_dim(first_low, dp_index * crops, crops, 0)
    pooled_grad = dot_right(own_low, head_first) / crop_tokens[:, None]

    out_grad, out_low, head_sums = call(
        head_back_body,
        (shape((rows, width), F32), shape((rows, width), BF16), shape((3, width), F32)),
        (block_out, feature_cotangent, crop_of_row, pooled_grad, norm_gains[2:3]),
    )
    normed_two_grad = None
    inner_parts, outer_parts, inner_sums = [None] * count, [None] * count, [None] * count
    order = [k for k in range(count) if k % 2] + [k for k in range(count) if not k % 2]
    for k in order:
        here = slice(k * hidden, (k + 1) * hidden)
        act_k, slope_k = act[:, here], slope[:, here]
        pre_grad = (dot_right(out_low, w_outer[k]) * slope_k.astype(F32)).astype(BF16)
        kind = BF16 if k % 2 else F32
        outer_parts[k] = dot_left(out_low, act_k).astype(kind)
        inner_parts[k] = dot_left(normed_two, pre_grad).astype(kind)
        inner_sums[k] = jnp.sum(pre_grad.astype(F32), axis=0)
        share = dot_right(pre_grad, w_inner[k])
        normed_two_grad = share if normed_two_grad is None else normed_two_grad + share
    outer_sum = scatter_sum(outer_parts, True)
    inner_sum = scatter_sum(inner_parts, False)
    mixed_grad, mixed_low, mixed_sums = call(
        functools.partial(mixed_back_body, windows),
        (shape((rows, width), F32), shape((padded_rows, width), BF16), shape((3, width), F32)),
        (mixed, out_grad, normed_two_grad, norm_gains[1:2]),
        scratch=[pltpu.VMEM((rows + 16, width), F32)],
    )
    input_grads, pair_grads, input_sums = [None] * count, [None] * count, [None] * count
    attend_parts, input_parts = [None] * count, [None] * count
    for k in order:
        input_grads[k], pair_grads[k], input_sums[k] = call(
            functools.partial(attend_back_body, heads, scale),
            (
                shape((padded_rows, 3 * quarter), BF16),
                shape((PAD, heads * PAD), F32),
                shape((1, 3 * quarter), F32),
            ),
            (mixed_low, w_att[k], q[k], k_[k], v[k], probs[k]),
            scratch=[pltpu.VMEM((padded_rows, quarter), BF16)],
        )
        kind = BF16 if k % 2 else F32
        attend_parts[k] = dot_left(mixed_low, attended[k]).astype(kind)
        input_parts[k] = dot_left(padded, input_grads[k]).astype(kind)
    joined = [jnp.concatenate([a, b], axis=1) for a, b in zip(input_parts, attend_parts)]
    joined_sum = scatter_sum(joined, False)
    tokens_grad, token_sums = call(
        functools.partial(tokens_back_body, windows, count),
        (shape((rows, width), F32), shape((2, width), F32)),
        (*input_grads, *w_in, tokens, mixed_grad, norm_gains[0:1]),
        scratch=[pltpu.VMEM((rows, width), F32)],
    )

    pair_grad = jnp.stack(pair_grads).reshape(count, PAD, heads, PAD)
    pair_grad = by_distance(pair_grad, "narrow").transpose(1, 3, 0, 2).reshape(PAD * PAD, count * heads)
    table_grad = lax.dot_general(
        table, pair_grad, (((0,), (0,)), ((), ())), precision=HIGH, preferred_element_type=F32
    )
    input_sum = by_distance(jnp.stack(input_sums).reshape(count, 3, quarter), "narrow")
    input_sum = input_sum.swapaxes(0, 1).reshape(3, count * quarter)
    inner_bias_sum = by_distance(jnp.stack(inner_sums), "narrow")
    pieces = [
        token_sums[0:1], mixed_sums[0:1], head_sums[0:1],
        token_sums[1:2], mixed_sums[2:3], mixed_sums[1:2], head_sums[2:3], head_sums[1:2],
        input_sum[0:1], input_sum[2:3],
        inner_bias_sum, table_grad,
    ]
    flat = jnp.concatenate([p.reshape(-1) for p in pieces])
    small = sum_over(flat, ("narrow", "dp"))
    gain_total = small[: 3 * width].reshape(3, width)
    offset_total = small[3 * width : 8 * width].reshape(5, width)
    bias_total = small[8 * width : 10 * width].reshape(2, width)
    inner_total = small[10 * width : 10 * width + hidden * count]
    table_total = small[10 * width + hidden * count :].reshape(table_grad.shape)

    logits = dot(units, columns_low)
    column_grad = dot_left(units, logit_cotangent)
    keep = (1 - first_epoch).astype(F32)[None, :]
    along = jnp.sum(column_grad * direction, axis=0, keepdims=True)
    gain_grad = (keep * column_inv * along)[0]
    direction_grad = (keep * prototype_gain) * (
        column_inv * column_grad - (column_inv**3 * along) * direction
    )

    def own(values):
        share = values.shape[1] // groups
        return lax.dynamic_slice_in_dim(values, dp_index * share, share, 1)

    own_first, own_second = own(first_low), own(second_low)
    own_embed = own(embed_grad)

    attend_sum = joined_sum[:, 3 * quarter :]
    input_total = jnp.stack([joined_sum[:, i * quarter : (i + 1) * quarter] for i in range(3)])
    return (
        features,
        logits,
        tokens_grad,
        input_total,
        bias_total,
        table_total,
        attend_sum.T,
        inner_sum,
        inner_total,
        outer_sum.T,
        gain_total,
        offset_total,
        dot_left(pooled, own_first),
        jnp.sum(own_first.astype(F32), axis=0),
        dot_left(first_act, own_second),
        jnp.sum(own_second.astype(F32), axis=0),
        dot_left(own(second_act), embed_low),
        jnp.sum(own_embed, axis=0),
        direction_grad,
        gain_grad,
    )


def solution(mesh):
    placed = (
        P(("dp", "narrow"), None),
        P(None, None, "narrow"),
        P(),
        P(),
        P("narrow", None),
        P(None, "narrow"),
        P(),
        P("narrow", None),
        P(),
        P(),
        P(),
        P(),
        P(),
        P(),
        P(),
        P(),
        P(None, ("dp", "narrow")),
        P(("dp", "narrow")),
        P("dp", None),
        P(("dp", "narrow")),
        P(("dp", "narrow"), None),
        P(None, ("dp", "narrow")),
    )
    return jax.shard_map(
        shards,
        mesh=mesh,
        in_specs=placed,
        out_specs=(
            P(("dp", "narrow"), None),
            P(None, ("dp", "narrow")),
            P(("dp", "narrow"), None),
            P(None, "dp", "narrow"),
            P(),
            P(),
            P("narrow", "dp"),
            P("dp", "narrow"),
            P(),
            P("narrow", "dp"),
            P(),
            P(),
            P(None, "dp"),
            P("dp"),
            P(None, "dp"),
            P("dp"),
            P("dp", None),
            P("dp"),
            P(None, ("dp", "narrow")),
            P(("dp", "narrow")),
        ),
        check_vma=False,
    )
```

time: 1420 us -> 554 us (0.39)
  waiting for transfers between devices: 842 us -> 167 us
  Pallas kernels: 0 us -> 164 us
  blocking collectives: 156 us -> 0 us
  matrix products: 236 us -> 91.1 us
  local copies, waits for them, and re-layouts: 113 us -> 40.6 us
  starting transfers between devices: 0.81 us -> 48.5 us
  between operations: 16.6 us -> 2.32 us
    reduce_scatter x9 -> x0, waiting for transfers between devices: 690 us -> none  [the longest x1 286 us: shards(): lax.psum_scatter(head_grads[2], 'dp', scatter_dimension=1, tiled=True)]
    ppermute x0 -> x46, waiting for transfers between devices: none -> 167 us  [swap(): lax.ppermute(values, axis, [(i, i ^ bit) for i in range(lax.axis_size(axi...]
    pallas_call x0 -> x14, Pallas kernels: none -> 164 us  [the longest x13 132 us: call(): pl.pallas_call(body, out_shape=outs, in_specs=[pl.BlockSpec(memory_space=...]
    all_gather x4 -> x0, waiting for transfers between devices: 152 us -> none  [the longest x1 39.1 us: shards(): lax.all_gather(out_grad.astype(jnp.bfloat16), 'narrow', axis=0, tiled=True)]
    dot_general x39 -> x38, matrix products: 230 us -> 91.1 us  [the longest x20 49.8 us: dot_left(): lax.dot_general(left, right, (((0,), (0,)), ((), ())), preferred_element_...]
    psum x3 -> x0, blocking collectives: 92.4 us -> none  [the longest x1 42.3 us: shards(): lax.psum((gain_stack, offset_stack, bias_whole, inner_bias_whole, table_w...]
    ppermute x0 -> x46, starting transfers between devices: none -> 48.5 us  [swap(): lax.ppermute(values, axis, [(i, i ^ bit) for i in range(lax.axis_size(axi...]
    convert_element_type x8 -> x10, local copies, waits for them, and re-layouts: 40.8 us -> 2.05 us  [halve_rows(): lax.dynamic_index_in_dim(folded, 1 - mine, 1, keepdims=False).astype(low)]
  transfers between devices with their start and end apart: 15 -> 46, of which waited for: 13 -> 23; matrix products, arithmetic and copies ran while one was open for 8% -> 17% of each run, Pallas kernels for 0% -> 21%
where the time goes in v1:
time: 554 us; the launch traced here: 549 us
  waiting for transfers between devices  167 us (30%)
  Pallas kernels  164 us (30%)
  matrix products  91.1 us (16%)
  starting transfers between devices  48.5 us (9%)
  local copies, waits for them, and re-layouts  40.6 us (7%)
  other arithmetic  36.2 us (7%)
    ppermute x46, waiting for transfers between devices, swap(): lax.ppermute(values, axis, [(i, i ^ bit) for i in range(lax.axis_size(axi...  167 us
    pallas_call x13, Pallas kernels, call(): pl.pallas_call(body, out_shape=outs, in_specs=[pl.BlockSpec(memory_space=...  132 us
    dot_general x20, matrix products, dot_left(): lax.dot_general(left, right, (((0,), (0,)), ((), ())), preferred_element_...  49.8 us
    ppermute x46, starting transfers between devices, swap(): lax.ppermute(values, axis, [(i, i ^ bit) for i in range(lax.axis_size(axi...  48.5 us
    pallas_call x1, Pallas kernels, shards(): pl.pallas_call(functools.partial(inner_body, blocks, count), grid=(steps,...  31.8 us
    dot_general x12, matrix products, dot_right(): lax.dot_general(left, right, (((1,), (1,)), ((), ())), preferred_element_...  27.8 us
  transfers between devices with their start and end apart: 46, of which 23 were waited for; matrix products, arithmetic and copies ran while one was open for 17% of the time, Pallas kernels for 21%

profile of v1, /device:TPU:0, one launch (start us, length us, event | category | flops | bytes accessed | tf_op | source)
XLA Modules:
  0.0 549.3 jit_solution(17270910641411480446)
XLA Ops:
  20.8 9.8 %collective-permute-done.4.refs_6_.weight = bf16[192,768]{1,0:T(8,128)(2,1)} collective-permute-done((bf16[192,768]{1,0:T(8,128)(2,1)}, bf16[192,768]{1,0:T(8,128)(2,1)}, u32[]{:S(2)}, u32[]{:S(2)}) %collective-permute-start.4) | collective-permute-done | bytes 294944 | tf_op jit(solution)/shard_map/ppermute | solution.py:293
  40.7 3.5 shard_map.365.padded
  45.0 9.5 %shard_map.366 = (bf16[1024,192]{1,0:T(8,128)(2,1)}, bf16[1024,192]{1,0:T(8,128)(2,1)}, bf16[1024,192]{1,0:T(8,128)(2,1)}, bf16[1024,384]{1,0:T(8,128)(2,1)}, bf16[1024,192]{1,0:T(8,128)(2,1)}) custom-call(bf16[1024,768]{1,0:T(8,128)(2,1)} %shard_map.365.padded, bf16[3,768,192]{2,1,0:T(8,128)(2,1)} %copy.109.weight.refs_4_, ...), custom_call_target="tpu_custom_call" | custom-call | tf_op jit(solution)/shard_map/pallas_call | solution.py:34
  55.2 48.9 %collective-permute-done.2 = bf16[3,768,192]{1,2,0:T(8,128)(2,1)} collective-permute-done((bf16[3,768,192]{1,2,0:T(8,128)(2,1)}, bf16[3,768,192]{1,2,0:T(8,128)(2,1)}, u32[]{:S(2)}, u32[]{:S(2)}) %collective-permute-start.2) | collective-permute-done | bytes 884768 | tf_op jit(solution)/shard_map/ppermute | solution.py:293
  109.4 9.6 %shard_map.367 = (bf16[1024,192]{1,0:T(8,128)(2,1)}, bf16[1024,192]{1,0:T(8,128)(2,1)}, bf16[1024,192]{1,0:T(8,128)(2,1)}, bf16[1024,384]{1,0:T(8,128)(2,1)}, bf16[1024,192]{1,0:T(8,128)(2,1)}) custom-call(bf16[1024,768]{1,0:T(8,128)(2,1)} %shard_map.365.padded, bf16[3,768,192]{2,1,0:T(8,128)(2,1)} %copy.110.weight.refs_5_, ...), custom_call_target="tpu_custom_call" | custom-call | tf_op jit(solution)/shard_map/pallas_call | solution.py:34
  121.3 9.5 %shard_map.368 = (bf16[1024,192]{1,0:T(8,128)(2,1)}, bf16[1024,192]{1,0:T(8,128)(2,1)}, bf16[1024,192]{1,0:T(8,128)(2,1)}, bf16[1024,384]{1,0:T(8,128)(2,1)}, bf16[1024,192]{1,0:T(8,128)(2,1)}) custom-call(bf16[1024,768]{1,0:T(8,128)(2,1)} %shard_map.365.padded, bf16[3,768,192]{2,1,0:T(8,128)(2,1)} %copy.111.weight.refs_6_, ...), custom_call_target="tpu_custom_call" | custom-call | tf_op jit(solution)/shard_map/pallas_call | solution.py:34
  133.1 9.8 %shard_map.369 = (bf16[1024,192]{1,0:T(8,128)(2,1)}, bf16[1024,192]{1,0:T(8,128)(2,1)}, bf16[1024,192]{1,0:T(8,128)(2,1)}, bf16[1024,384]{1,0:T(8,128)(2,1)}, bf16[1024,192]{1,0:T(8,128)(2,1)}) custom-call(bf16[1024,768]{1,0:T(8,128)(2,1)} %shard_map.365.padded, bf16[3,768,192]{2,1,0:T(8,128)(2,1)} %copy.112.weight.refs_7_, ...), custom_call_target="tpu_custom_call" | custom-call | tf_op jit(solution)/shard_map/pallas_call | solution.py:34
  143.0 16.8 %collective-permute-done.5.refs_7_.weight = bf16[192,768]{1,0:T(8,128)(2,1)} collective-permute-done((bf16[192,768]{1,0:T(8,128)(2,1)S(1)}, bf16[192,768]{1,0:T(8,128)(2,1)}, u32[]{:S(2)}, u32[]{:S(2)}) %collective-permute-start.5) | collective-permute-done | bytes 294944 | tf_op jit(solution)/shard_map/ppermute | solution.py:293
  159.8 7.8 %shard_map.370 = (f32[784,768]{1,0:T(8,128)}, bf16[784,768]{1,0:T(8,128)(2,1)}) custom-call(bf16[1024,192]{1,0:T(8,128)(2,1)} %get-tuple-element.67.refs_0_, bf16[1024,192]{1,0:T(8,128)(2,1)} %get-tuple-element.68.refs_1_, bf16[1024,192]{1,0:T(8,128)(2,1)} %get-tuple-element.69.refs_2_, bf16[1024,192]{1,0:T(8,128)(2,1)} %get-tuple-element.70.refs_3_, ...), custom_call_target="tpu_custom_call" | custom-call | tf_op jit(solution)/shard_map/pallas_call | solution.py:34
  167.7 31.8 %shard_map.371 = (bf16[784,3072]{1,0:T(8,128)(2,1)}, bf16[784,3072]{1,0:T(8,128)(2,1)}, f32[784,768]{1,0:T(8,128)}, bf16[784,768]{1,0:T(8,128)(2,1)}, f32[4,768]{1,0:T(4,128)}) custom-call(bf16[784,768]{1,0:T(8,128)(2,1)} %get-tuple-element.71.refs_0_, f32[784,768]{1,0:T(8,128)} %get-tuple-element.72.refs_1_.mixed, f32[4,1,768]{2,1,0:T(1,128)} %bitcast.227, ...), custom_call_target="tpu_custom_call" | custom-call | tf_op jit(solution)/shard_map/pallas_call | solution.py:520
  219.6 6.2 %multiply_convert_fusion.4 = (bf16[32,2048]{1,0:T(8,128)(2,1)S(1)}, f32[32,2048]{1,0:T(8,128)}) fusion(f32[2048]{0:T(1024)S(1)} %copy-done.56, bf16[32,2048]{1,0:T(8,128)(2,1)S(1)} %get-tuple-element.230, bf16[2048,2048]{1,0:T(8,128)(2,1)} %param.34), kind=kOutput, calls=%fused_computation.100 | convolution fusion | flops 272760832 | bytes 8921088 | tf_op jit(solution)/shard_map/dot_general | solution.py:21
  240.6 3.7 fusion.7
  251.1 6.0 %fusion.74 = f32[32,2048]{1,0:T(8,128)S(1)} fusion(bf16[32,2048]{1,0:T(8,128)(2,1)S(1)} %add_convert_fusion.3, bf16[2048,2048]{1,0:T(8,128)(2,1)} %param.34), kind=kOutput, calls=%fused_computation.238 | convolution fusion | flops 268435456 | bytes 8781824 | tf_op jit(solution)/shard_map/dot_general | solution.py:29
  258.8 6.7 %shard_map.372 = (f32[784,768]{1,0:T(8,128)}, bf16[784,768]{1,0:T(8,128)(2,1)}, f32[3,768]{1,0:T(4,128)}) custom-call(f32[784,768]{1,0:T(8,128)} %get-tuple-element.75.block_out, bf16[784,768]{1,0:T(8,128)(2,1)} %cotangent.1, s32[784,1]{1,0:T(8,128)} %broadcast_in_dim.22.refs_12_.crop, f32[4,768]{1,0:T(4,128)} %convolution_divide_fusion.pooled_grad, ...), custom_call_target="tpu_custom_call" | custom-call | tf_op jit(solution)/shard_map/pallas_call | solution.py:34
  265.5 4.5 convolution_convert_fusion.1
  270.0 4.2 fusion.14
  303.0 4.0 add_add_fusion.normed_grad
  307.0 7.2 %shard_map.373 = (f32[784,768]{1,0:T(8,128)}, bf16[1024,768]{1,0:T(8,128)(2,1)}, f32[3,768]{1,0:T(4,128)}) custom-call(f32[784,768]{1,0:T(8,128)} %get-tuple-element.72.refs_1_.mixed, f32[784,768]{1,0:T(8,128)} %get-tuple-element.76.out_grad, f32[784,768]{1,0:T(8,128)} %add_add_fusion.normed_grad, f32[1,768]{1,0:T(1,128)} %copy-done.47), custom_call_target="tpu_custom_call" | custom-call | tf_op jit(solution)/shard_map/pallas_call | solution.py:34
  320.7 9.6 %shard_map.374 = (bf16[1024,576]{1,0:T(8,128)(2,1)}, f32[64,384]{1,0:T(8,128)}, f32[1,576]{1,0:T(1,128)}) custom-call(bf16[1024,768]{1,0:T(8,128)(2,1)} %get-tuple-element.79.low, bf16[192,768]{1,0:T(8,128)(2,1)} %weight.2, bf16[1024,192]{1,0:T(8,128)(2,1)} %get-tuple-element.80.q_in, bf16[1024,192]{1,0:T(8,128)(2,1)} %get-tuple-element.81.k_in, ...), custom_call_target="tpu_custom_call" | custom-call | tf_op jit(solution)/shard_map/pallas_call | solution.py:34
  330.3 9.8 %shard_map.377 = (bf16[1024,576]{1,0:T(8,128)(2,1)}, f32[64,384]{1,0:T(8,128)}, f32[1,576]{1,0:T(1,128)}) custom-call(bf16[1024,768]{1,0:T(8,128)(2,1)} %get-tuple-element.79.low, bf16[192,768]{1,0:T(8,128)(2,1)} %collective-permute-done.5.refs_7_.weight, bf16[1024,192]{1,0:T(8,128)(2,1)} %get-tuple-element.95.q_in, ...), custom_call_target="tpu_custom_call" | custom-call | tf_op jit(solution)/shard_map/pallas_call | solution.py:34
  340.1 9.6 %shard_map.376 = (bf16[1024,576]{1,0:T(8,128)(2,1)}, f32[64,384]{1,0:T(8,128)}, f32[1,576]{1,0:T(1,128)}) custom-call(bf16[1024,768]{1,0:T(8,128)(2,1)} %get-tuple-element.79.low, bf16[192,768]{1,0:T(8,128)(2,1)} %collective-permute-done.4.refs_6_.weight, bf16[1024,192]{1,0:T(8,128)(2,1)} %get-tuple-element.90.q_in, ...), custom_call_target="tpu_custom_call" | custom-call | tf_op jit(solution)/shard_map/pallas_call | solution.py:34
  349.7 9.6 %shard_map.375 = (bf16[1024,576]{1,0:T(8,128)(2,1)}, f32[64,384]{1,0:T(8,128)}, f32[1,576]{1,0:T(1,128)}) custom-call(bf16[1024,768]{1,0:T(8,128)(2,1)} %get-tuple-element.79.low, bf16[192,768]{1,0:T(8,128)(2,1)} %copy-done.22, bf16[1024,192]{1,0:T(8,128)(2,1)} %get-tuple-element.85.q_in, bf16[1024,192]{1,0:T(8,128)(2,1)} %get-tuple-element.86.k_in, ...), custom_call_target="tpu_custom_call" | custom-call | tf_op jit(solution)/shard_map/pallas_call | solution.py:34
  365.6 3.5 convolution_convert_fusion.5
  376.1 29.6 %shard_map.378 = (f32[784,768]{1,0:T(8,128)}, f32[2,768]{1,0:T(2,128)}) custom-call(bf16[1024,576]{1,0:T(8,128)(2,1)} %get-tuple-element.84.refs_0_, bf16[1024,576]{1,0:T(8,128)(2,1)} %get-tuple-element.89.refs_1_, bf16[1024,576]{1,0:T(8,128)(2,1)} %get-tuple-element.94.refs_2_, bf16[1024,576]{1,0:T(8,128)(2,1)} %get-tuple-element.99.refs_3_, ...), custom_call_target="tpu_custom_call" | custom-call | tf_op jit(solution)/shard_map/pallas_call | solution.py:34
  408.9 4.6 fusion.83
  441.7 8.9 %collective-permute-done.42 = bf16[4,96,768]{2,1,0:T(8,128)(2,1)S(1)} collective-permute-done((bf16[4,96,768]{2,1,0:T(8,128)(2,1)S(1)}, bf16[4,96,768]{2,1,0:T(8,128)(2,1)S(1)}, u32[]{:S(2)}, u32[]{:S(2)}) %collective-permute-start.42) | collective-permute-done | bytes 589856 | tf_op jit(solution)/shard_map/ppermute | solution.py:293
  467.1 25.4 %collective-permute-done.43 = bf16[4,96,768]{2,1,0:T(8,128)(2,1)} collective-permute-done((bf16[4,96,768]{2,1,0:T(8,128)(2,1)S(1)}, bf16[4,96,768]{2,1,0:T(8,128)(2,1)}, u32[]{:S(2)}, u32[]{:S(2)}) %collective-permute-start.43) | collective-permute-done | bytes 589856 | tf_op jit(solution)/shard_map/ppermute | solution.py:293
  499.2 3.2 collective-permute-done.44
  502.6 12.8 %collective-permute-done.35 = bf16[8,96,768]{2,1,0:T(8,128)(2,1)S(1)} collective-permute-done((bf16[8,96,768]{2,1,0:T(8,128)(2,1)S(1)}, bf16[8,96,768]{2,1,0:T(8,128)(2,1)S(1)}, u32[]{:S(2)}, u32[]{:S(2)}) %collective-permute-start.35) | collective-permute-done | bytes 1179680 | tf_op jit(solution)/shard_map/ppermute | solution.py:293
  519.8 9.1 %collective-permute-done.36 = bf16[4,96,768]{2,1,0:T(8,128)(2,1)S(1)} collective-permute-done((bf16[4,96,768]{2,1,0:T(8,128)(2,1)S(1)}, bf16[4,96,768]{2,1,0:T(8,128)(2,1)S(1)}, u32[]{:S(2)}, u32[]{:S(2)}) %collective-permute-start.36) | collective-permute-done | bytes 589856 | tf_op jit(solution)/shard_map/ppermute | solution.py:293
  531.0 6.7 %collective-permute-done.37 = bf16[2,96,768]{2,1,0:T(8,128)(2,1)S(1)} collective-permute-done((bf16[2,96,768]{2,1,0:T(8,128)(2,1)S(1)}, bf16[2,96,768]{2,1,0:T(8,128)(2,1)S(1)}, u32[]{:S(2)}, u32[]{:S(2)}) %collective-permute-start.37) | collective-permute-done | bytes 294944 | tf_op jit(solution)/shard_map/ppermute | solution.py:293
  541.9 5.1 collective-permute-done.38
  (407 shorter events, 200.0 us)
Async XLA Ops:
  0.7 31.7 %collective-permute-start = (bf16[3,768,192]{1,2,0:T(8,128)(2,1)}, bf16[3,768,192]{1,2,0:T(8,128)(2,1)}, u32[]{:S(2)}, u32[]{:S(2)}) collective-permute-start(bf16[3,768,192]{1,2,0:T(8,128)(2,1)} %param.23), channel_id=1, source_target_pairs={{0,1},{1,0},{2,3},{3,2},{4,5},{5,4},{6,7},{7,6},{8,9},{9,8},{10,11... | collective-permute-start | bytes 2654216 | tf_op jit(solution)/shard_map/ppermute | solution.py:293
  1.2 31.5 %collective-permute-start.1 = (bf16[3,768,192]{1,2,0:T(8,128)(2,1)}, bf16[3,768,192]{1,2,0:T(8,128)(2,1)}, u32[]{:S(2)}, u32[]{:S(2)}) collective-permute-start(bf16[3,768,192]{1,2,0:T(8,128)(2,1)} %param.23), channel_id=1, source_target_pairs={{0,2},{1,3},{2,0},{3,1},{4,6},{5,7},{6,4},{7,5},{8,10},{9,11},{10,... | collective-permute-start | bytes 2654216 | tf_op jit(solution)/shard_map/ppermute | solution.py:293
  3.8 12.6 %collective-permute-start.3 = (bf16[192,768]{1,0:T(8,128)(2,1)}, bf16[192,768]{1,0:T(8,128)(2,1)S(1)}, u32[]{:S(2)}, u32[]{:S(2)}) collective-permute-start(bf16[192,768]{1,0:T(8,128)(2,1)} %weight.2), channel_id=1, source_target_pairs={{0,1},{1,0},{2,3},{3,2},{4,5},{5,4},{6,7},{7,6},{8,9},{9,8},{10,11... | collective-permute-start | bytes 884744 | tf_op jit(solution)/shard_map/ppermute | solution.py:293
  3.9 30.5 %collective-permute-start.9 = (bf16[768,768]{1,0:T(8,128)(2,1)}, bf16[768,768]{1,0:T(8,128)(2,1)}, u32[]{:S(2)}, u32[]{:S(2)}) collective-permute-start(bf16[768,768]{1,0:T(8,128)(2,1)} %refs_7_.1), channel_id=1, source_target_pairs={{0,1},{1,0},{2,3},{3,2},{4,5},{5,4},{6,7},{7,6},{8,9},{9,8},{10,11... | collective-permute-start | bytes 3538952 | tf_op jit(solution)/shard_map/ppermute | solution.py:293
  4.3 30.4 %collective-permute-start.6 = (bf16[768,768]{1,0:T(8,128)(2,1)}, bf16[768,768]{1,0:T(8,128)(2,1)}, u32[]{:S(2)}, u32[]{:S(2)}) collective-permute-start(bf16[768,768]{1,0:T(8,128)(2,1)} %refs_3_.1), channel_id=1, source_target_pairs={{0,1},{1,0},{2,3},{3,2},{4,5},{5,4},{6,7},{7,6},{8,9},{9,8},{10,11... | collective-permute-start | bytes 3538952 | tf_op jit(solution)/shard_map/ppermute | solution.py:293
  16.4 14.2 %collective-permute-start.4 = (bf16[192,768]{1,0:T(8,128)(2,1)}, bf16[192,768]{1,0:T(8,128)(2,1)}, u32[]{:S(2)}, u32[]{:S(2)}) collective-permute-start(bf16[192,768]{1,0:T(8,128)(2,1)} %weight.2), channel_id=1, source_target_pairs={{0,2},{1,3},{2,0},{3,1},{4,6},{5,7},{6,4},{7,5},{8,10},{9,11},{10,... | collective-permute-start | bytes 884744 | tf_op jit(solution)/shard_map/ppermute | solution.py:293
  30.6 137.0 %collective-permute-start.10 = (bf16[768,768]{1,0:T(8,128)(2,1)}, bf16[768,768]{1,0:T(8,128)(2,1)}, u32[]{:S(2)}, u32[]{:S(2)}) collective-permute-start(bf16[768,768]{1,0:T(8,128)(2,1)} %refs_7_.1), channel_id=1, source_target_pairs={{0,2},{1,3},{2,0},{3,1},{4,6},{5,7},{6,4},{7,5},{8,10},{9,11},{10,... | collective-permute-start | bytes 3538952 | tf_op jit(solution)/shard_map/ppermute | solution.py:293
  32.4 135.2 %collective-permute-start.7 = (bf16[768,768]{1,0:T(8,128)(2,1)}, bf16[768,768]{1,0:T(8,128)(2,1)}, u32[]{:S(2)}, u32[]{:S(2)}) collective-permute-start(bf16[768,768]{1,0:T(8,128)(2,1)} %refs_3_.1), channel_id=1, source_target_pairs={{0,2},{1,3},{2,0},{3,1},{4,6},{5,7},{6,4},{7,5},{8,10},{9,11},{10,... | collective-permute-start | bytes 3538952 | tf_op jit(solution)/shard_map/ppermute | solution.py:293
  32.7 71.4 %collective-permute-start.2 = (bf16[3,768,192]{1,2,0:T(8,128)(2,1)}, bf16[3,768,192]{1,2,0:T(8,128)(2,1)}, u32[]{:S(2)}, u32[]{:S(2)}) collective-permute-start(bf16[3,768,192]{1,2,0:T(8,128)(2,1)} %collective-permute-done), channel_id=1, source_target_pairs={{0,2},{1,3},{2,0},{3,1},{4,6},{5,7},{6,4},{7,5},{8,10},{9,11},{10,... | collective-permute-start | bytes 2654216 | tf_op jit(solution)/shard_map/ppermute | solution.py:293
  34.4 133.2 %collective-permute-start.11 = (bf16[768,768]{1,0:T(8,128)(2,1)}, bf16[768,768]{1,0:T(8,128)(2,1)}, u32[]{:S(2)}, u32[]{:S(2)}) collective-permute-start(bf16[768,768]{1,0:T(8,128)(2,1)} %collective-permute-done.9.refs_8_), channel_id=1, source_target_pairs={{0,2},{1,3},{2,0},{3,1},{4,6},{5,7},{6,4},{7,5},{8,10},{9,11},{10,... | collective-permute-start | bytes 3538952 | tf_op jit(solution)/shard_map/ppermute | solution.py:293
  34.7 133.0 %collective-permute-start.8 = (bf16[768,768]{1,0:T(8,128)(2,1)}, bf16[768,768]{1,0:T(8,128)(2,1)}, u32[]{:S(2)}, u32[]{:S(2)}) collective-permute-start(bf16[768,768]{1,0:T(8,128)(2,1)} %collective-permute-done.6.refs_4_), channel_id=1, source_target_pairs={{0,2},{1,3},{2,0},{3,1},{4,6},{5,7},{6,4},{7,5},{8,10},{9,11},{10,... | collective-permute-start | bytes 3538952 | tf_op jit(solution)/shard_map/ppermute | solution.py:293
  104.0 55.7 %collective-permute-start.5 = (bf16[192,768]{1,0:T(8,128)(2,1)S(1)}, bf16[192,768]{1,0:T(8,128)(2,1)}, u32[]{:S(2)}, u32[]{:S(2)}) collective-permute-start(bf16[192,768]{1,0:T(8,128)(2,1)S(1)} %copy-done.23), channel_id=1, source_target_pairs={{0,2},{1,3},{2,0},{3,1},{4,6},{5,7},{6,4},{7,5},{8,10},{9,11},{10,... | collective-permute-start | bytes 884744 | tf_op jit(solution)/shard_map/ppermute | solution.py:293
  320.1 114.3 %collective-permute-start.39 = (bf16[8,96,768]{2,1,0:T(8,128)(2,1)}, bf16[8,96,768]{2,1,0:T(8,128)(2,1)}, u32[]{:S(2)}, u32[]{:S(2)}) collective-permute-start(bf16[8,96,768]{2,1,0:T(8,128)(2,1)} %bitcast.65), channel_id=1, source_target_pairs={{0,1},{1,0},{2,3},{3,2},{4,5},{5,4},{6,7},{7,6},{8,9},{9,8},{10,11... | collective-permute-start | bytes 3538952 | tf_op jit(solution)/shard_map/ppermute | solution.py:293
  320.2 109.1 %collective-permute-start.41 = (bf16[8,96,768]{2,1,0:T(8,128)(2,1)}, bf16[8,96,768]{2,1,0:T(8,128)(2,1)}, u32[]{:S(2)}, u32[]{:S(2)}) collective-permute-start(bf16[8,96,768]{2,1,0:T(8,128)(2,1)} %bitcast.70), channel_id=1, source_target_pairs={{0,1},{1,0},{2,3},{3,2},{4,5},{5,4},{6,7},{7,6},{8,9},{9,8},{10,11... | collective-permute-start | bytes 3538952 | tf_op jit(solution)/shard_map/ppermute | solution.py:293
  320.7 142.5 %collective-permute-start.34 = (bf16[8,96,768]{2,1,0:T(8,128)(2,1)}, bf16[8,96,768]{2,1,0:T(8,128)(2,1)}, u32[]{:S(2)}, u32[]{:S(2)}) collective-permute-start(bf16[8,96,768]{2,1,0:T(8,128)(2,1)} %bitcast.56), channel_id=1, source_target_pairs={{0,1},{1,0},{2,3},{3,2},{4,5},{5,4},{6,7},{7,6},{8,9},{9,8},{10,11... | collective-permute-start | bytes 3538952 | tf_op jit(solution)/shard_map/ppermute | solution.py:293
  406.8 9.4 %collective-permute-start.28 = (f32[14808]{0:T(1024)S(1)}, f32[14808]{0:T(1024)S(1)}, u32[]{:S(2)}, u32[]{:S(2)}) collective-permute-start(f32[14808]{0:T(1024)S(1)} %constant_dynamic-update-slice_fusion), channel_id=1, source_target_pairs={{0,1},{1,0},{2,3},{3,2},{4,5},{5,4},{6,7},{7,6},{8,9},{9,8},{10,11... | collective-permute-start | bytes 177704 | tf_op jit(solution)/shard_map/ppermute | solution.py:293
  408.9 29.8 %collective-permute-start.23 = (bf16[8,96,768]{2,1,0:T(8,128)(2,1)}, bf16[8,96,768]{2,1,0:T(8,128)(2,1)}, u32[]{:S(2)}, u32[]{:S(2)}) collective-permute-start(bf16[8,96,768]{2,1,0:T(8,128)(2,1)} %bitcast.222), channel_id=1, source_target_pairs={{0,1},{1,0},{2,3},{3,2},{4,5},{5,4},{6,7},{7,6},{8,9},{9,8},{10,11... | collective-permute-start | bytes 3538952 | tf_op jit(solution)/shard_map/ppermute | solution.py:293
  429.3 66.4 %collective-permute-start.22 = (bf16[8,96,768]{2,1,0:T(8,128)(2,1)}, bf16[8,96,768]{2,1,0:T(8,128)(2,1)}, u32[]{:S(2)}, u32[]{:S(2)}) collective-permute-start(bf16[8,96,768]{2,1,0:T(8,128)(2,1)} %bitcast.221), channel_id=1, source_target_pairs={{0,1},{1,0},{2,3},{3,2},{4,5},{5,4},{6,7},{7,6},{8,9},{9,8},{10,11... | collective-permute-start | bytes 3538952 | tf_op jit(solution)/shard_map/ppermute | solution.py:293
  429.3 23.0 %collective-permute-start.32 = (f32[14808]{0:T(1024)S(1)}, f32[14808]{0:T(1024)S(1)}, u32[]{:S(2)}, u32[]{:S(2)}) collective-permute-start(f32[14808]{0:T(1024)S(1)} %add.360), channel_id=1, source_target_pairs={{0,16},{4,20},{8,24},{12,28},{16,0},{20,4},{24,8},{28,12},{1,17},{... | collective-permute-start | bytes 177704 | tf_op jit(solution)/shard_map/ppermute | solution.py:293
  434.4 16.2 %collective-permute-start.42 = (bf16[4,96,768]{2,1,0:T(8,128)(2,1)S(1)}, bf16[4,96,768]{2,1,0:T(8,128)(2,1)S(1)}, u32[]{:S(2)}, u32[]{:S(2)}) collective-permute-start(bf16[4,96,768]{2,1,0:T(8,128)(2,1)S(1)} %fusion.26), channel_id=1, source_target_pairs={{0,4},{4,0},{8,12},{12,8},{16,20},{20,16},{24,28},{28,24},{1,5},{5... | collective-permute-start | bytes 1769480 | tf_op jit(solution)/shard_map/ppermute | solution.py:293
  438.6 26.9 %collective-permute-start.40 = (bf16[4,96,768]{2,1,0:T(8,128)(2,1)}, bf16[4,96,768]{2,1,0:T(8,128)(2,1)}, u32[]{:S(2)}, u32[]{:S(2)}) collective-permute-start(bf16[4,96,768]{2,1,0:T(8,128)(2,1)} %fusion.24), channel_id=1, source_target_pairs={{0,4},{4,0},{8,12},{12,8},{16,20},{20,16},{24,28},{28,24},{1,5},{5... | collective-permute-start | bytes 1769480 | tf_op jit(solution)/shard_map/ppermute | solution.py:293
  450.7 45.0 %collective-permute-start.24 = (bf16[8,96,768]{2,1,0:T(8,128)(2,1)}, bf16[8,96,768]{2,1,0:T(8,128)(2,1)}, u32[]{:S(2)}, u32[]{:S(2)}) collective-permute-start(bf16[8,96,768]{2,1,0:T(8,128)(2,1)} %add_convert_fusion.1), channel_id=1, source_target_pairs={{0,2},{1,3},{2,0},{3,1},{4,6},{5,7},{6,4},{7,5},{8,10},{9,11},{10,... | collective-permute-start | bytes 3538952 | tf_op jit(solution)/shard_map/ppermute | solution.py:293
  452.3 40.2 %collective-permute-start.43 = (bf16[4,96,768]{2,1,0:T(8,128)(2,1)S(1)}, bf16[4,96,768]{2,1,0:T(8,128)(2,1)}, u32[]{:S(2)}, u32[]{:S(2)}) collective-permute-start(bf16[4,96,768]{2,1,0:T(8,128)(2,1)S(1)} %fusion.16), channel_id=1, source_target_pairs={{0,2},{1,3},{2,0},{3,1},{4,6},{5,7},{6,4},{7,5},{8,10},{9,11},{10,... | collective-permute-start | bytes 1769480 | tf_op jit(solution)/shard_map/ppermute | solution.py:293
  463.1 39.5 %collective-permute-start.33 = (bf16[8,96,768]{2,1,0:T(8,128)(2,1)}, bf16[8,96,768]{2,1,0:T(8,128)(2,1)S(1)}, u32[]{:S(2)}, u32[]{:S(2)}) collective-permute-start(bf16[8,96,768]{2,1,0:T(8,128)(2,1)} %bitcast.242), channel_id=1, source_target_pairs={{0,1},{1,0},{2,3},{3,2},{4,5},{5,4},{6,7},{7,6},{8,9},{9,8},{10,11... | collective-permute-start | bytes 3538952 | tf_op jit(solution)/shard_map/ppermute | solution.py:293
  465.5 49.8 %collective-permute-start.35 = (bf16[8,96,768]{2,1,0:T(8,128)(2,1)S(1)}, bf16[8,96,768]{2,1,0:T(8,128)(2,1)S(1)}, u32[]{:S(2)}, u32[]{:S(2)}) collective-permute-start(bf16[8,96,768]{2,1,0:T(8,128)(2,1)S(1)} %add_convert_fusion), channel_id=1, source_target_pairs={{0,2},{1,3},{2,0},{3,1},{4,6},{5,7},{6,4},{7,5},{8,10},{9,11},{10,... | collective-permute-start | bytes 3538952 | tf_op jit(solution)/shard_map/ppermute | solution.py:293
  494.1 8.4 %collective-permute-start.44 = (bf16[2,96,768]{2,1,0:T(8,128)(2,1)S(1)}, bf16[2,96,768]{2,1,0:T(8,128)(2,1)S(1)}, u32[]{:S(2)}, u32[]{:S(2)}) collective-permute-start(bf16[2,96,768]{2,1,0:T(8,128)(2,1)S(1)} %fusion.30), channel_id=1, source_target_pairs={{0,8},{4,12},{8,0},{12,4},{16,24},{20,28},{24,16},{28,20},{1,9},{5... | collective-permute-start | bytes 884744 | tf_op jit(solution)/shard_map/ppermute | solution.py:293
  497.7 20.4 %collective-permute-start.25 = (bf16[4,96,768]{2,1,0:T(8,128)(2,1)S(1)}, bf16[4,96,768]{2,1,0:T(8,128)(2,1)S(1)}, u32[]{:S(2)}, u32[]{:S(2)}) collective-permute-start(bf16[4,96,768]{2,1,0:T(8,128)(2,1)S(1)} %fusion.25), channel_id=1, source_target_pairs={{0,4},{4,0},{8,12},{12,8},{16,20},{20,16},{24,28},{28,24},{1,5},{5... | collective-permute-start | bytes 1769480 | tf_op jit(solution)/shard_map/ppermute | solution.py:293
  502.5 14.8 %collective-permute-start.45 = (bf16[1,96,768]{2,1,0:T(8,128)(2,1)S(1)}, bf16[1,96,768]{2,1,0:T(8,128)(2,1)S(1)}, u32[]{:S(2)}, u32[]{:S(2)}) collective-permute-start(bf16[1,96,768]{2,1,0:T(8,128)(2,1)S(1)} %dynamic-slice_convert_fusion.5), channel_id=1, source_target_pairs={{0,16},{4,20},{8,24},{12,28},{16,0},{20,4},{24,8},{28,12},{1,17},{... | collective-permute-start | bytes 442376 | tf_op jit(solution)/shard_map/ppermute | solution.py:293
  515.8 13.1 %collective-permute-start.36 = (bf16[4,96,768]{2,1,0:T(8,128)(2,1)S(1)}, bf16[4,96,768]{2,1,0:T(8,128)(2,1)S(1)}, u32[]{:S(2)}, u32[]{:S(2)}) collective-permute-start(bf16[4,96,768]{2,1,0:T(8,128)(2,1)S(1)} %fusion.23), channel_id=1, source_target_pairs={{0,4},{4,0},{8,12},{12,8},{16,20},{20,16},{24,28},{28,24},{1,5},{5... | collective-permute-start | bytes 1769480 | tf_op jit(solution)/shard_map/ppermute | solution.py:293
  518.3 12.3 %collective-permute-start.26 = (bf16[2,96,768]{2,1,0:T(8,128)(2,1)S(1)}, bf16[2,96,768]{2,1,0:T(8,128)(2,1)S(1)}, u32[]{:S(2)}, u32[]{:S(2)}) collective-permute-start(bf16[2,96,768]{2,1,0:T(8,128)(2,1)S(1)} %fusion.28), channel_id=1, source_target_pairs={{0,8},{4,12},{8,0},{12,4},{16,24},{20,28},{24,16},{28,20},{1,9},{5... | collective-permute-start | bytes 884744 | tf_op jit(solution)/shard_map/ppermute | solution.py:293
  529.0 8.7 %collective-permute-start.37 = (bf16[2,96,768]{2,1,0:T(8,128)(2,1)S(1)}, bf16[2,96,768]{2,1,0:T(8,128)(2,1)S(1)}, u32[]{:S(2)}, u32[]{:S(2)}) collective-permute-start(bf16[2,96,768]{2,1,0:T(8,128)(2,1)S(1)} %fusion.29), channel_id=1, source_target_pairs={{0,8},{4,12},{8,0},{12,4},{16,24},{20,28},{24,16},{28,20},{1,9},{5... | collective-permute-start | bytes 884744 | tf_op jit(solution)/shard_map/ppermute | solution.py:293
  530.6 9.7 %collective-permute-start.27 = (bf16[1,96,768]{2,1,0:T(8,128)(2,1)S(1)}, bf16[1,96,768]{2,1,0:T(8,128)(2,1)S(1)}, u32[]{:S(2)}, u32[]{:S(2)}) collective-permute-start(bf16[1,96,768]{2,1,0:T(8,128)(2,1)S(1)} %dynamic-slice_convert_fusion.7), channel_id=1, source_target_pairs={{0,16},{4,20},{8,24},{12,28},{16,0},{20,4},{24,8},{28,12},{1,17},{... | collective-permute-start | bytes 442376 | tf_op jit(solution)/shard_map/ppermute | solution.py:293
  (89 other events, 1187.0 us)
